TPU v7x, 512 devices: a whole 4x8x8 slice. The times are simulated.
512 devices in a mesh: nodes: 32 (over x_lo, z, core), tensor: 16 (over y, x_hi).
Axes of the slice: x: 4 (x_hi: 2, x_lo: 2; x = x_hi * 2 + x_lo), y: 8, z: 8, core: 2. Of those that a mesh axis runs over, the one named last changes fastest.
Arguments:
- node_states: bfloat16 [32768, 1024], P(('nodes', 'tensor')), may hold values from -6 to 6
- norm_gain: float32 [1024], replicated, may hold values from 0.1 to 1.9
- input_weight: bfloat16 [3072, 1024], P('tensor'), may hold values from -3 to 3, as said below
- output_weight: bfloat16 [1024, 1024], P('tensor'), may hold values from -0.1875 to 0.1875
- expander_bias: float32 [4, 16], P(None, 'tensor'), may hold values from 3 to 6
- local_blocks: int32 [128, 4], P('nodes'), may hold values from 0 to 127, as said below
- expander_source: int32 [4, 32768], P(None, 'nodes'), may hold values from 0 to 32767, as said below
Outputs:
- layer_output: bfloat16 [32768, 1024], P(('nodes', 'tensor'))
Inputs may be any that keep to these rules, and one draw needn't show every extreme that they name: `local_blocks`: row g lists block g first, then 4 - 1 other distinct blocks among the 8 consecutive blocks that start at min(max(g - 4, 0), 120). `expander_source`: each of the 4 rows is a permutation of the 32768 nodes. With partitions of 1024 consecutive nodes, in every round exactly 32 nodes of any partition take their expander source from any given partition. `input_weight`: rows h * 3 * 64 onward hold head h's query, key and value rows in that order.
All inputs are finite; a program needn't handle non-finite values.
Results may differ from a plain program's by a relative error of at most 0.0051.
Values may be sent and summed in bfloat16 or wider, within the bound.
A program may use at most 64 MiB of HBM per device.

v0:
```python
import math

import jax
import jax.numpy as jnp
from jax import lax
from jax.sharding import PartitionSpec as P

D = 1024
HEAD = 64
BLOCK = 256
NEIGH = 4
ROUNDS = 4


def padded(block, sides, width):
    for axis, dim in sides:
        count = lax.axis_size(axis)
        forward = [(i, i + 1) for i in range(count - 1)]
        backward = [(target, source) for source, target in forward]
        low = lax.ppermute(
            lax.slice_in_dim(block, block.shape[dim] - width, None, axis=dim), axis, forward
        )
        high = lax.ppermute(lax.slice_in_dim(block, 0, width, axis=dim), axis, backward)
        block = jnp.concatenate([low, block, high], axis=dim)
    return block


def per_device(
    node_states,
    norm_gain,
    input_weight,
    output_weight,
    expander_bias,
    local_blocks,
    expander_source,
):
    tensor_count = lax.axis_size("tensor")
    own_rows = node_states.shape[0]
    row_count = own_rows * tensor_count
    partitions = lax.axis_size("nodes")
    heads_here = input_weight.shape[0] // (3 * HEAD)
    blocks_here = row_count // BLOCK
    peer_rows = row_count // partitions
    score_scale = 1.0 / math.sqrt(HEAD)
    kv_width = heads_here * 2 * HEAD
    contract_last = (((1,), (1,)), ((), ()))
    widened = lax.all_gather(node_states, "tensor", axis=0, tiled=True).astype(jnp.float32)
    inverse_rms = lax.rsqrt(jnp.sum(widened * widened, axis=1) / D + 1e-05)
    scaled = (widened * norm_gain).astype(jnp.bfloat16)
    totals = lax.dot_general(
        scaled, input_weight, contract_last, preferred_element_type=jnp.float32
    )
    projected = (totals * inverse_rms[:, None]).astype(jnp.bfloat16)
    projected = projected.reshape(row_count, heads_here, 3 * HEAD)
    queries = projected[:, :, :HEAD]
    padded_queries = jnp.concatenate([queries, jnp.zeros_like(queries)], axis=2)
    key_values = projected[:, :, HEAD:].reshape(row_count, kv_width)
    extended = padded(key_values, (("nodes", 0),), row_count)
    extended_blocks = extended.reshape(3 * blocks_here, BLOCK * kv_width)
    first_block = lax.axis_index("nodes") * blocks_here - blocks_here
    relative = local_blocks - first_block
    block_ids = jnp.arange(3 * blocks_here, dtype=jnp.int32)
    owners = expander_source // row_count
    within = expander_source % row_count
    order = jnp.argsort(owners, axis=1, stable=True)
    wanted = jnp.take_along_axis(within, order, axis=1).reshape(ROUNDS, partitions, peer_rows)
    collected = []
    for round_index in range(ROUNDS):
        collected.append(
            lax.all_to_all(
                key_values[
                    lax.all_to_all(
                        wanted[round_index : round_index + 1],
                        "nodes",
                        split_axis=1,
                        concat_axis=1,
                        tiled=True,
                    )
                ],
                "nodes",
                split_axis=1,
                concat_axis=1,
                tiled=True,
            )
        )
    received = jnp.concatenate(collected, axis=0)
    received = received.reshape(ROUNDS, row_count, kv_width)
    restore = jnp.argsort(order, axis=1)
    far_rows = jnp.take_along_axis(received, restore[:, :, None], axis=1).reshape(
        ROUNDS, row_count, heads_here, 2 * HEAD
    )
    query_tiles_local = padded_queries.reshape(blocks_here, BLOCK, heads_here, 2 * HEAD)
    bias_rows = jnp.transpose(expander_bias, (1, 0))

    def attend_group(group_index):
        first_row = group_index * 2
        group_queries = lax.dynamic_slice_in_dim(query_tiles_local, first_row, 2, 0)
        group_relative = lax.dynamic_slice_in_dim(relative, first_row, 2, 0)
        selector = (group_relative[:, :, None] == block_ids[None, None, :]).astype(jnp.bfloat16)
        group_blocks = jnp.einsum(
            "bnc,ce->bne", selector, extended_blocks, preferred_element_type=jnp.float32
        ).astype(jnp.bfloat16)
        group_blocks = group_blocks.reshape(2, NEIGH, BLOCK, heads_here, 2 * HEAD)
        group_far = lax.dynamic_slice_in_dim(far_rows, first_row * BLOCK, 2 * BLOCK, 1).reshape(
            ROUNDS, 2, BLOCK, heads_here, 2 * HEAD
        )
        nearby_scores = (
            jnp.einsum(
                "bqhe,bnkhe->bhqnk", group_queries, group_blocks, preferred_element_type=jnp.float32
            )
            * score_scale
        )
        scores_far = (
            jnp.einsum(
                "bqhe,rbqhe->bhqr", group_queries, group_far, preferred_element_type=jnp.float32
            )
            * score_scale
        )
        scores_far = scores_far + bias_rows[None, :, None, :]
        highest = jnp.maximum(jnp.max(nearby_scores, axis=(3, 4)), jnp.max(scores_far, axis=3))
        exponent_nearby = jnp.exp(nearby_scores - highest[:, :, :, None, None])
        exponent_distant = jnp.exp(scores_far - highest[:, :, :, None])
        total = jnp.sum(exponent_nearby, axis=(3, 4)) + jnp.sum(exponent_distant, axis=3)
        blended_output = jnp.einsum(
            "bhqnk,bnkhe->bqhe",
            exponent_nearby.astype(jnp.bfloat16),
            group_blocks,
            preferred_element_type=jnp.float32,
        )
        blended_output = blended_output + jnp.einsum(
            "bhqr,rbqhe->bqhe",
            exponent_distant.astype(jnp.bfloat16),
            group_far,
            preferred_element_type=jnp.float32,
        )
        value_part = blended_output[:, :, :, HEAD:]
        return (value_part / jnp.transpose(total, (0, 2, 1))[:, :, :, None]).astype(jnp.bfloat16)

    attended = lax.map(attend_group, jnp.arange(blocks_here // 2, dtype=jnp.int32))
    head_outputs = attended.reshape(row_count, heads_here * HEAD)
    node_rows = lax.all_to_all(head_outputs, "tensor", split_axis=0, concat_axis=1, tiled=True)
    projected_out = jnp.dot(
        node_rows,
        lax.all_gather(output_weight, "tensor", axis=0, tiled=True),
        preferred_element_type=jnp.float32,
    )
    return (node_states.astype(jnp.float32) + projected_out).astype(jnp.bfloat16)


def solution(mesh):
    in_specs = (
        P(("nodes", "tensor"), None),
        P(),
        P("tensor", None),
        P("tensor", None),
        P(None, "tensor"),
        P("nodes", None),
        P(None, "nodes"),
    )
    out_specs = P(("nodes", "tensor"), None)
    return jax.shard_map(
        per_device, mesh=mesh, in_specs=in_specs, out_specs=out_specs, check_vma=False
    )
```

profile of v0, /device:TPU:1, one launch (start us, length us, event | category | flops | bytes accessed | tf_op | source)
XLA Modules:
  0.0 287.1 jit_solution(15986033676408083352)
XLA Ops:
  10.0 3.9 %sort.37.cloned.1.call-done = (s32[4,1024]{1,0:T(4,128)}, s32[4,1024]{1,0:T(4,128)}) async-done(((s32[4,1024]{1,0:T(4,128)}, s32[4,1024]{1,0:T(4,128)}), (s32[4,1024]{1,0:T(4,128)}, s32[4,1024]{1,0:T(4,128)})) %sort.37.cloned.1.call-update) | async-done | bytes 32784 | tf_op jit(solution)/shard_map/jit(argsort)/sort | solution.py:65
  14.6 34.9 %gather_fusion.4 = s32[4096]{0:T(1024)S(1)} fusion(s32[4,1024]{1,0:T(4,128)S(1)} %get-tuple-element.200, s32[4096]{0:T(1024)S(1)} %bitcast.127), kind=kCustom, calls=%fused_computation.4 | custom fusion | bytes 65536 | tf_op jit(solution)/shard_map/jit(take_along_axis)/gather | solution.py:66
  50.3 12.9 %all-to-all-start = ((s32[1,32,32]{2,0,1:T(1,128)}), s32[1,32,32]{2,0,1:T(1,128)S(1)}, u32[]{:S(2)}, u32[]{:S(2)}) async-start(s32[1,32,32]{2,0,1:T(1,128)} %bitcast.5), calls=%async_computation | async-start | bytes 32768 | tf_op jit(solution)/shard_map/all_to_all | solution.py:72
  63.9 7.1 %all-to-all-done = s32[1,32,32]{2,0,1:T(1,128)S(1)} async-done(((s32[1,32,32]{2,0,1:T(1,128)}), s32[1,32,32]{2,0,1:T(1,128)S(1)}, u32[]{:S(2)}, u32[]{:S(2)}) %all-to-all-start) | async-done | bytes 4128 | tf_op jit(solution)/shard_map/all_to_all | solution.py:72
  71.0 4.3 %all-to-all-start.2 = ((s32[1,32,32]{2,0,1:T(1,128)}), s32[1,32,32]{2,0,1:T(1,128)S(1)}, u32[]{:S(2)}, u32[]{:S(2)}) async-start(s32[1,32,32]{2,0,1:T(1,128)} %bitcast.8), calls=%async_computation.2 | async-start | bytes 32768 | tf_op jit(solution)/shard_map/all_to_all | solution.py:72
  76.6 6.6 %all-to-all-done.2 = s32[1,32,32]{2,0,1:T(1,128)S(1)} async-done(((s32[1,32,32]{2,0,1:T(1,128)}), s32[1,32,32]{2,0,1:T(1,128)S(1)}, u32[]{:S(2)}, u32[]{:S(2)}) %all-to-all-start.2) | async-done | bytes 4128 | tf_op jit(solution)/shard_map/all_to_all | solution.py:72
  83.2 4.3 %all-to-all-start.4 = ((s32[1,32,32]{2,0,1:T(1,128)}), s32[1,32,32]{2,0,1:T(1,128)S(1)}, u32[]{:S(2)}, u32[]{:S(2)}) async-start(s32[1,32,32]{2,0,1:T(1,128)} %bitcast.11), calls=%async_computation.4 | async-start | bytes 32768 | tf_op jit(solution)/shard_map/all_to_all | solution.py:72
  87.7 18.5 %all-gather.3.cloned.1.call-done = bf16[1024,1024]{1,0:T(8,128)(2,1)} async-done(((bf16[64,1024]{1,0:T(8,128)(2,1)}), bf16[1024,1024]{1,0:T(8,128)(2,1)}) %all-gather.3.cloned.1.call-update) | async-done | bytes 2097168 | tf_op jit(solution)/shard_map/all_gather | solution.py:47
  109.4 11.7 %all-to-all-start.6 = ((s32[1,32,32]{2,0,1:T(1,128)}), s32[1,32,32]{2,0,1:T(1,128)S(1)}, u32[]{:S(2)}, u32[]{:S(2)}) async-start(s32[1,32,32]{2,0,1:T(1,128)} %bitcast.14), calls=%async_computation.6 | async-start | bytes 32768 | tf_op jit(solution)/shard_map/all_to_all | solution.py:72
  121.4 4.3 %gather_fusion = bf16[1024,128]{1,0:T(8,128)(2,1)} fusion(bf16[1024,128]{1,0:T(8,128)(2,1)S(1)} %copy.50, s32[1024]{0:T(1024)S(1)} %broadcast_clamp_fusion.3), kind=kCustom, calls=%fused_computation | custom fusion | bytes 528384 | tf_op jit(solution)/shard_map/gather | solution.py:71
  128.8 5.2 %all-to-all-start.1 = ((bf16[1,32,32,128]{3,2,0,1:T(8,128)(2,1)}), bf16[1,32,32,128]{3,2,0,1:T(8,128)(2,1)S(1)}, u32[]{:S(2)}, u32[]{:S(2)}) async-start(bf16[1,32,32,128]{3,2,0,1:T(8,128)(2,1)} %bitcast.7), calls=%async_computation.1 | async-start | bytes 524288 | tf_op jit(solution)/shard_map/all_to_all | solution.py:70
  134.1 4.3 %gather_fusion.1 = bf16[1024,128]{1,0:T(8,128)(2,1)} fusion(bf16[1024,128]{1,0:T(8,128)(2,1)S(1)} %copy.50, s32[1024]{0:T(1024)S(1)} %broadcast_clamp_fusion.2), kind=kCustom, calls=%fused_computation.1 | custom fusion | bytes 528384 | tf_op jit(solution)/shard_map/gather | solution.py:71
  138.3 7.6 %all-to-all-done.1 = bf16[1,32,32,128]{3,2,0,1:T(8,128)(2,1)S(1)} async-done(((bf16[1,32,32,128]{3,2,0,1:T(8,128)(2,1)}), bf16[1,32,32,128]{3,2,0,1:T(8,128)(2,1)S(1)}, u32[]{:S(2)}, u32[]{:S(2)}) %all-to-all-start.1) | async-done | bytes 262176 | tf_op jit(solution)/shard_map/all_to_all | solution.py:70
  145.9 5.0 %all-to-all-start.3 = ((bf16[1,32,32,128]{3,2,0,1:T(8,128)(2,1)}), bf16[1,32,32,128]{3,2,0,1:T(8,128)(2,1)S(1)}, u32[]{:S(2)}, u32[]{:S(2)}) async-start(bf16[1,32,32,128]{3,2,0,1:T(8,128)(2,1)} %bitcast.10), calls=%async_computation.3 | async-start | bytes 524288 | tf_op jit(solution)/shard_map/all_to_all | solution.py:70
  152.5 4.3 %gather_fusion.2 = bf16[1024,128]{1,0:T(8,128)(2,1)} fusion(bf16[1024,128]{1,0:T(8,128)(2,1)S(1)} %copy.50, s32[1024]{0:T(1024)S(1)} %broadcast_clamp_fusion.1), kind=kCustom, calls=%fused_computation.2 | custom fusion | bytes 528384 | tf_op jit(solution)/shard_map/gather | solution.py:71
  156.7 6.2 %all-to-all-done.3 = bf16[1,32,32,128]{3,2,0,1:T(8,128)(2,1)S(1)} async-done(((bf16[1,32,32,128]{3,2,0,1:T(8,128)(2,1)}), bf16[1,32,32,128]{3,2,0,1:T(8,128)(2,1)S(1)}, u32[]{:S(2)}, u32[]{:S(2)}) %all-to-all-start.3) | async-done | bytes 262176 | tf_op jit(solution)/shard_map/all_to_all | solution.py:70
  163.0 5.0 %all-to-all-start.5 = ((bf16[1,32,32,128]{3,2,0,1:T(8,128)(2,1)}), bf16[1,32,32,128]{3,2,0,1:T(8,128)(2,1)S(1)}, u32[]{:S(2)}, u32[]{:S(2)}) async-start(bf16[1,32,32,128]{3,2,0,1:T(8,128)(2,1)} %bitcast.13), calls=%async_computation.5 | async-start | bytes 524288 | tf_op jit(solution)/shard_map/all_to_all | solution.py:70
  168.7 3.5 %collective-permute-start = (bf16[1024,128]{0,1:T(8,128)(2,1)S(1)}, bf16[1024,128]{0,1:T(8,128)(2,1)S(1)}, u32[]{:S(2)}, u32[]{:S(2)}) collective-permute-start(bf16[1024,128]{0,1:T(8,128)(2,1)S(1)} %get-tuple-element.198), channel_id=1, source_target_pairs={{0,16},{16,32},{32,48},{48,64},{64,80},{80,96},{96,112},{112,128},... | collective-permute-start | bytes 786440 | tf_op jit(solution)/shard_map/ppermute | solution.py:20
  175.0 4.3 %gather_fusion.3 = bf16[1024,128]{1,0:T(8,128)(2,1)} fusion(bf16[1024,128]{1,0:T(8,128)(2,1)S(1)} %copy.50, s32[1024]{0:T(1024)S(1)} %broadcast_clamp_fusion), kind=kCustom, calls=%fused_computation.3 | custom fusion | bytes 528384 | tf_op jit(solution)/shard_map/gather | solution.py:71
  180.0 9.0 %all-to-all-start.7 = ((bf16[1,32,32,128]{3,2,0,1:T(8,128)(2,1)}), bf16[1,32,32,128]{3,2,0,1:T(8,128)(2,1)S(1)}, u32[]{:S(2)}, u32[]{:S(2)}) async-start(bf16[1,32,32,128]{3,2,0,1:T(8,128)(2,1)} %bitcast.16), calls=%async_computation.7 | async-start | bytes 524288 | tf_op jit(solution)/shard_map/all_to_all | solution.py:70
  191.8 9.1 %all-to-all-done.7 = bf16[1,32,32,128]{3,2,0,1:T(8,128)(2,1)S(1)} async-done(((bf16[1,32,32,128]{3,2,0,1:T(8,128)(2,1)}), bf16[1,32,32,128]{3,2,0,1:T(8,128)(2,1)S(1)}, u32[]{:S(2)}, u32[]{:S(2)}) %all-to-all-start.7) | async-done | bytes 262176 | tf_op jit(solution)/shard_map/all_to_all | solution.py:70
  201.1 21.7 %gather_fusion.5 = bf16[4096,128]{1,0:T(8,128)(2,1)S(1)} fusion(bf16[4,1024,128]{2,1,0:T(8,128)(2,1)S(1)} %bitcast.128, s32[4096]{0:T(1024)S(1)} %bitcast.126), kind=kCustom, calls=%fused_computation.5 | custom fusion | bytes 2129920 | tf_op jit(solution)/shard_map/jit(take_along_axis)/gather | solution.py:89
  225.6 34.1 %while.13 = (s32[]{:T(128)}, bf16[2,2,256,1,64]{2,1,0,4,3:T(2,128)(2,1)}, s32[2]{0:T(128)}, s32[4,4]{1,0:T(4,128)}, bf16[12,32768]{1,0:T(8,128)(2,1)}, /*index=5...) while((s32[]{:T(128)}, ...), condition=%wide.region_8.9_spmd.clone, body=%wide.region_3.8_spmd.clone.sunk | while | flops 280544352 | bytes 14979993 | solution.py:139
  261.2 15.5 %all_to_all.59 = bf16[16,2,2048]{2,1,0:T(2,128)(2,1)S(1)} all-to-all(bf16[16,2,2048]{2,1,0:T(2,128)(2,1)S(1)} %reshape.291), channel_id=1, replica_groups=mesh['nodes'=32,'tensor'=16] {'tensor'}, dimensions={0} | all-to-all | bytes 262144 | tf_op jit(solution)/shard_map/all_to_all | solution.py:141
  (119 shorter events, 60.3 us)
Async XLA Ops:
  7.4 101.1 %copy-start = (bf16[192,1024]{1,0:T(8,128)(2,1)S(1)}, bf16[192,1024]{1,0:T(8,128)(2,1)}, u32[]{:S(2)}) copy-start(bf16[192,1024]{1,0:T(8,128)(2,1)} %param.11) | copy-start | bytes 1179652
  7.4 6.5 %sort.37.cloned.1.call-start = ((), (), s32[]{:S(2)}) async-start(), calls=%async_computation.11 | async-start | bytes 98336 | tf_op jit(solution)/shard_map/jit(argsort)/sort | solution.py:65
  9.4 96.8 %all-gather.3.cloned.1.call-start = ((), (), s32[]{:S(2)}) async-start(), calls=%async_computation.9 | async-start | bytes 2228224 | tf_op jit(solution)/shard_map/all_gather | solution.py:47
  14.6 35.0 %copy-start.3 = (s32[4,1024]{1,0:T(4,128)S(1)}, s32[4,1024]{1,0:T(4,128)}, u32[]{:S(2)}) copy-start(s32[4,1024]{1,0:T(4,128)} %get-tuple-element.120) | copy-start | bytes 49156
  49.5 59.0 %copy-start.7 = (f32[1024]{0:T(1024)S(1)}, f32[1024]{0:T(1024)}, u32[]{:S(2)}) copy-start(f32[1024]{0:T(1024)} %param.10) | copy-start | bytes 12292
  50.3 20.7 %all-to-all-start = ((s32[1,32,32]{2,0,1:T(1,128)}), s32[1,32,32]{2,0,1:T(1,128)S(1)}, u32[]{:S(2)}, u32[]{:S(2)}) async-start(s32[1,32,32]{2,0,1:T(1,128)} %bitcast.5), calls=%async_computation | async-start | bytes 32768 | tf_op jit(solution)/shard_map/all_to_all | solution.py:72
  71.0 12.2 %all-to-all-start.2 = ((s32[1,32,32]{2,0,1:T(1,128)}), s32[1,32,32]{2,0,1:T(1,128)S(1)}, u32[]{:S(2)}, u32[]{:S(2)}) async-start(s32[1,32,32]{2,0,1:T(1,128)} %bitcast.8), calls=%async_computation.2 | async-start | bytes 32768 | tf_op jit(solution)/shard_map/all_to_all | solution.py:72
  83.2 26.2 %all-to-all-start.4 = ((s32[1,32,32]{2,0,1:T(1,128)}), s32[1,32,32]{2,0,1:T(1,128)S(1)}, u32[]{:S(2)}, u32[]{:S(2)}) async-start(s32[1,32,32]{2,0,1:T(1,128)} %bitcast.11), calls=%async_computation.4 | async-start | bytes 32768 | tf_op jit(solution)/shard_map/all_to_all | solution.py:72
  106.2 2.3 copy-start.2
  108.5 12.6 %copy-start.6 = (pred[128]{0:T(512)(128)(4,1)S(1)}, pred[128]{0:T(512)(128)(4,1)}, u32[]{:S(2)}) copy-start(pred[128]{0:T(512)(128)(4,1)} %constant.118.clone.1) | copy-start | bytes 388
  109.4 19.4 %all-to-all-start.6 = ((s32[1,32,32]{2,0,1:T(1,128)}), s32[1,32,32]{2,0,1:T(1,128)S(1)}, u32[]{:S(2)}, u32[]{:S(2)}) async-start(s32[1,32,32]{2,0,1:T(1,128)} %bitcast.14), calls=%async_computation.6 | async-start | bytes 32768 | tf_op jit(solution)/shard_map/all_to_all | solution.py:72
  128.8 17.1 %all-to-all-start.1 = ((bf16[1,32,32,128]{3,2,0,1:T(8,128)(2,1)}), bf16[1,32,32,128]{3,2,0,1:T(8,128)(2,1)S(1)}, u32[]{:S(2)}, u32[]{:S(2)}) async-start(bf16[1,32,32,128]{3,2,0,1:T(8,128)(2,1)} %bitcast.7), calls=%async_computation.1 | async-start | bytes 524288 | tf_op jit(solution)/shard_map/all_to_all | solution.py:70
  138.3 29.7 %copy-start.5 = (s32[4,4]{1,0:T(4,128)S(1)}, s32[4,4]{1,0:T(4,128)}, u32[]{:S(2)}) copy-start(s32[4,4]{1,0:T(4,128)} %param.14) | copy-start | bytes 196
  145.9 17.1 %all-to-all-start.3 = ((bf16[1,32,32,128]{3,2,0,1:T(8,128)(2,1)}), bf16[1,32,32,128]{3,2,0,1:T(8,128)(2,1)S(1)}, u32[]{:S(2)}, u32[]{:S(2)}) async-start(bf16[1,32,32,128]{3,2,0,1:T(8,128)(2,1)} %bitcast.10), calls=%async_computation.3 | async-start | bytes 524288 | tf_op jit(solution)/shard_map/all_to_all | solution.py:70
  150.9 23.2 %sort.39.cloned.1.call-start = ((), (), s32[]{:S(2)}) async-start(), calls=%async_computation.12 | async-start | bytes 98336 | tf_op jit(solution)/shard_map/jit(argsort)/sort | solution.py:88
  151.7 125.2 %all-gather.5.cloned.1.call-start = ((), (), s32[]{:S(2)}) async-start(), calls=%async_computation.10 | async-start | bytes 2228224 | tf_op jit(solution)/shard_map/all_gather | solution.py:144
  163.0 17.1 %all-to-all-start.5 = ((bf16[1,32,32,128]{3,2,0,1:T(8,128)(2,1)}), bf16[1,32,32,128]{3,2,0,1:T(8,128)(2,1)S(1)}, u32[]{:S(2)}, u32[]{:S(2)}) async-start(bf16[1,32,32,128]{3,2,0,1:T(8,128)(2,1)} %bitcast.13), calls=%async_computation.5 | async-start | bytes 524288 | tf_op jit(solution)/shard_map/all_to_all | solution.py:70
  168.7 21.2 %collective-permute-start = (bf16[1024,128]{0,1:T(8,128)(2,1)S(1)}, bf16[1024,128]{0,1:T(8,128)(2,1)S(1)}, u32[]{:S(2)}, u32[]{:S(2)}) collective-permute-start(bf16[1024,128]{0,1:T(8,128)(2,1)S(1)} %get-tuple-element.198), channel_id=1, source_target_pairs={{0,16},{16,32},{32,48},{48,64},{64,80},{80,96},{96,112},{112,128},... | collective-permute-start | bytes 786440 | tf_op jit(solution)/shard_map/ppermute | solution.py:20
  172.2 17.6 %collective-permute-start.1 = (bf16[1024,128]{0,1:T(8,128)(2,1)S(1)}, bf16[1024,128]{0,1:T(8,128)(2,1)S(1)}, u32[]{:S(2)}, u32[]{:S(2)}) collective-permute-start(bf16[1024,128]{0,1:T(8,128)(2,1)S(1)} %get-tuple-element.198), channel_id=1, source_target_pairs={{16,0},{32,16},{48,32},{64,48},{80,64},{96,80},{112,96},{128,112},... | collective-permute-start | bytes 786440 | tf_op jit(solution)/shard_map/ppermute | solution.py:23
  174.2 14.8 %copy-start.4 = (s32[4,1024]{1,0:T(4,128)S(1)}, s32[4,1024]{1,0:T(4,128)}, u32[]{:S(2)}) copy-start(s32[4,1024]{1,0:T(4,128)} %get-tuple-element.121) | copy-start | bytes 49156
  180.0 20.9 %all-to-all-start.7 = ((bf16[1,32,32,128]{3,2,0,1:T(8,128)(2,1)}), bf16[1,32,32,128]{3,2,0,1:T(8,128)(2,1)S(1)}, u32[]{:S(2)}, u32[]{:S(2)}) async-start(bf16[1,32,32,128]{3,2,0,1:T(8,128)(2,1)} %bitcast.16), calls=%async_computation.7 | async-start | bytes 524288 | tf_op jit(solution)/shard_map/all_to_all | solution.py:70
  240.3 1.7 copy-start.1
  257.3 1.7 copy-start.1
Sparse Core Ops, SparseCore 0:
  10.7 2.8 sort.41.cloned.1.call-done
  154.4 4.4 sort.43.cloned.1.call-done
  (2 shorter events, 0.0 us)
Sparse Core Ops, SparseCore 1:
  13.1 93.1 all-gather.2
  155.3 85.3 all-gather.4
where the time goes:
time: 289 us; the launch traced here: 287 us
  local copies, waits for them, and re-layouts  101 us (35%)
  starting transfers between devices  62.9 us (22%)
  waiting for transfers between devices  60.1 us (21%)
  matrix products  16.6 us (6%)
  blocking collectives  15.5 us (5%)
  between operations  15.2 us (5%)
  other arithmetic  13 us (4%)
    gather x2, local copies, waits for them, and re-layouts, per_device(): jnp.take_along_axis(within, order, axis=1)  34.9 us
    all_to_all x4, starting transfers between devices, per_device(): lax.all_to_all(wanted[round_index:round_index + 1], 'nodes', split_axis=1...  33.1 us
    all_to_all x4, starting transfers between devices, per_device(): lax.all_to_all(key_values[lax.all_to_all(wanted[round_index:round_index +...  24.2 us
    all_to_all x4, waiting for transfers between devices, per_device(): lax.all_to_all(key_values[lax.all_to_all(wanted[round_index:round_index +...  23.7 us
    gather x1, local copies, waits for them, and re-layouts, per_device(): jnp.take_along_axis(received, restore[:, :, None], axis=1)  21.7 us
    all_gather x1, waiting for transfers between devices, per_device(): lax.all_gather(node_states, 'tensor', axis=0, tiled=True)  18.5 us
    gather x4, local copies, waits for them, and re-layouts, per_device(): key_values[lax.all_to_all(wanted[round_index:round_index + 1], 'nodes', s...  17.1 us
    all_to_all x4, waiting for transfers between devices, per_device(): lax.all_to_all(wanted[round_index:round_index + 1], 'nodes', split_axis=1...  16.8 us
  transfers between devices with their start and end apart: 12, of which 8 were waited for; matrix products, arithmetic and copies ran while one was open for 42% of the time, Pallas kernels for 0%

commit v1 on v0

v1 whole, which is shorter than its diff:
```python
import functools
import math

import jax
import jax.numpy as jnp
from jax import lax
from jax.experimental import pallas as pl
from jax.experimental.pallas import tpu as pltpu
from jax.sharding import PartitionSpec as P

D = 1024
HEAD = 64
BLOCK = 256
NEIGH = 4
ROUNDS = 4
EPS = 1e-05

BF16 = jnp.bfloat16
F32 = jnp.float32
MESH = pl.DeviceIdType.MESH
NT = (((1,), (1,)), ((), ()))


def iota(shape, dim):
    return lax.broadcasted_iota(jnp.int32, shape, dim)


def kernel(
    parts,
    peers,
    x_ref,
    gain_ref,
    win_ref,
    wout_ref,
    bias_ref,
    blocks_ref,
    src_ref,
    out_ref,
    xg,
    kvx,
    qs,
    reqs,
    reqr,
    posr,
    pick,
    place,
    snd,
    rcv,
    far,
    oloc,
    mloc,
    lloc,
    att,
    atts,
    attr,
    woutg,
    x_send,
    x_recv,
    w_send,
    w_recv,
    c_send,
    c_recv,
    r_send,
    r_recv,
    e_send,
    e_recv,
    n_send,
    n_recv,
    a_send,
    a_recv,
):
    own = x_ref.shape[0]
    rows = own * peers
    ring = peers // 2
    per = rows // parts
    blocks_here = rows // BLOCK
    p = lax.axis_index("nodes")
    t = lax.axis_index("tensor")
    y, xh = t // 2, t % 2
    core = p % 2
    other_core = p + 1 - 2 * core

    def node_peer(d):
        return (p + d) % parts

    def tensor_peer(d):
        return (t + d) % peers

    barrier = pltpu.get_barrier_semaphore()

    @pl.loop(1, parts)
    def _(d):
        pl.semaphore_signal(barrier, inc=1, device_id={"nodes": node_peer(d)}, device_id_type=MESH)

    @pl.loop(1, peers)
    def _(d):
        pl.semaphore_signal(
            barrier, inc=1, device_id={"tensor": tensor_peer(d)}, device_id_type=MESH
        )

    pl.semaphore_wait(barrier, parts + peers - 2)

    up = ((y + 1) % ring) * 2 + xh
    down = ((y + ring - 1) % ring) * 2 + xh
    across = y * 2 + 1 - xh

    def slot(k, column):
        side = xh if column == 0 else 1 - xh
        return ((y + ring - k) % ring) * 2 + side

    def x_copy(index, source, at, target):
        return pltpu.make_async_remote_copy(
            src_ref=source,
            dst_ref=xg.at[at],
            send_sem=x_send.at[index],
            recv_sem=x_recv.at[at],
            device_id={"tensor": target},
            device_id_type=MESH,
        )

    half = own // 2
    own_half = pl.ds(pl.multiple_of(core * half, half), half)
    other_half = pl.ds(pl.multiple_of((1 - core) * half, half), half)

    def w_copy(index, source, at, target):
        return pltpu.make_async_remote_copy(
            src_ref=source,
            dst_ref=woutg.at[at, own_half],
            send_sem=w_send.at[index],
            recv_sem=w_recv.at[at],
            device_id={"tensor": target},
            device_id_type=MESH,
        )

    def c_copy(at, part):
        return pltpu.make_async_remote_copy(
            src_ref=woutg.at[at, part],
            dst_ref=woutg.at[at, part],
            send_sem=c_send.at[at],
            recv_sem=c_recv.at[at],
            device_id={"nodes": other_core},
            device_id_type=MESH,
        )

    def ring_stages(make, first, gathered, arrived):
        sent = []

        def send(source, at, target):
            copy = make(len(sent), source, at, target)
            copy.start()
            sent.append(copy)

        def wait(at):
            make(0, gathered(at), at, up).wait_recv()

        send(first, t, up)
        send(first, t, down)
        send(first, t, across)
        yield
        s = slot(0, 1)
        wait(s)
        send(gathered(s), s, up)
        send(gathered(s), s, down)
        arrived(s)
        yield
        last = ring // 2
        for k in range(1, last + 1):
            got = []
            for column in range(2):
                if k < last or column == 0:
                    s = slot(k, column)
                    wait(s)
                    if k < last - 1 or (k == last - 1 and column == 0):
                        send(gathered(s), s, up)
                    got.append(s)
                if k < last or column == 1:
                    s = slot(ring - k, column)
                    wait(s)
                    if k < last - 1 or (k == last - 1 and column == 1):
                        send(gathered(s), s, down)
                    got.append(s)
            for s in got:
                arrived(s)
            yield
        for copy in sent:
            copy.wait_send()

    gain = gain_ref[...]
    wide_lane = iota((own, 2 * HEAD), 1)

    def project(states, at):
        wide = states.astype(F32)
        inverse = lax.rsqrt(jnp.sum(wide * wide, axis=1, keepdims=True) / D + EPS)
        scaled = (wide * gain).astype(BF16)
        totals = lax.dot_general(scaled, win_ref[...], NT, preferred_element_type=F32) * inverse
        start = pl.multiple_of(at * own, own)
        query = totals[:, : 2 * HEAD].astype(BF16).astype(F32) * (1.0 / math.sqrt(HEAD))
        qs[pl.ds(start, own)] = jnp.where(wide_lane < HEAD, query, 0.0).astype(BF16)
        inside = pl.multiple_of(at % (BLOCK // own) * own, own)
        kvx[blocks_here + at // (BLOCK // own), pl.ds(inside, own)] = totals[:, HEAD:].astype(BF16)

    states_ring = ring_stages(
        x_copy, x_ref, lambda at: xg.at[at], lambda at: project(xg[at], at)
    )
    next(states_ring)

    src = src_ref[...]
    owner = lax.shift_right_logical(src, rows.bit_length() - 1)
    within = (src & (rows - 1)).astype(F32)
    high = jnp.floor(within * (1.0 / per))
    low = within - high * per
    owner_row = iota((parts, rows), 0)
    belongs = [owner[r : r + 1] == owner_row for r in range(ROUNDS)]
    before = jnp.where(iota((rows, rows), 0) < iota((rows, rows), 1), 1.0, 0.0).astype(BF16)
    member = jnp.concatenate([jnp.where(b, 1.0, 0.0) for b in belongs], axis=0).astype(BF16)
    counts = jnp.dot(member, before, preferred_element_type=F32)
    slot_row = iota((ROUNDS * per, rows), 0).astype(F32)
    wanted_high = jnp.zeros((parts, ROUNDS * per), F32)
    wanted_low = jnp.zeros((parts, ROUNDS * per), F32)
    for r in range(ROUNDS):
        rank = jnp.sum(
            jnp.where(belongs[r], counts[r * parts : (r + 1) * parts], 0.0), axis=0, keepdims=True
        )
        position = owner[r : r + 1].astype(F32) * per + rank
        for c in range(rows // 128):
            posr[r * (rows // 128) + c] = position[:, c * 128 : (c + 1) * 128]
        chosen = jnp.where(slot_row == rank + r * per, 1.0, 0.0).astype(BF16)
        wanted_high += lax.dot_general(
            jnp.where(belongs[r], high[r : r + 1], 0.0).astype(BF16),
            chosen,
            NT,
            preferred_element_type=F32,
        )
        wanted_low += lax.dot_general(
            jnp.where(belongs[r], low[r : r + 1], 0.0).astype(BF16),
            chosen,
            NT,
            preferred_element_type=F32,
        )
    wanted = wanted_high * per + wanted_low
    for o in range(parts):
        reqs[o] = wanted[o : o + 1]

    def r_copy(peer, at):
        return pltpu.make_async_remote_copy(
            src_ref=reqs.at[peer],
            dst_ref=reqr.at[at],
            send_sem=r_send.at[peer],
            recv_sem=r_recv.at[at],
            device_id={"nodes": peer},
            device_id_type=MESH,
        )

    @pl.loop(1, parts)
    def _(d):
        r_copy(node_peer(d), p).start()

    reqr[p] = reqs[p]

    diagonal = iota((128, 128), 0) == iota((128, 128), 1)
    lane_index = iota((128, rows), 1).astype(F32)

    def one_hot(row):
        column = jnp.sum(jnp.where(diagonal, row, 0.0), axis=1, keepdims=True)
        return jnp.where(lane_index == column, 1.0, 0.0).astype(BF16)

    project(x_ref[...], t)
    next(states_ring)
    next(states_ring)

    @pl.loop(1, parts)
    def _(d):
        r_copy(node_peer(d), node_peer(d)).wait_recv()

    @pl.loop(0, parts)
    def _(i):
        pick[i] = one_hot(reqr[i])

    next(states_ring)

    @pl.loop(0, parts)
    def _(i):
        place[i] = one_hot(posr[i])

    for _ in states_ring:
        pass

    following, preceding = node_peer(1), node_peer(parts - 1)
    mine = kvx.at[pl.ds(blocks_here, blocks_here)]

    def n_copy(which, target):
        return pltpu.make_async_remote_copy(
            src_ref=mine,
            dst_ref=kvx.at[pl.ds(2 * blocks_here * which, blocks_here)],
            send_sem=n_send.at[which],
            recv_sem=n_recv.at[which],
            device_id={"nodes": target},
            device_id_type=MESH,
        )

    neighbours = [n_copy(0, following), n_copy(1, preceding)]
    for copy in neighbours:
        copy.start()

    woutg[t] = wout_ref[...]
    weight_ring = ring_stages(
        w_copy,
        wout_ref.at[own_half],
        lambda at: woutg.at[at, own_half],
        lambda at: c_copy(at, own_half).start(),
    )
    next(weight_ring)

    def e_copy(peer, at):
        return pltpu.make_async_remote_copy(
            src_ref=snd.at[peer],
            dst_ref=rcv.at[:, at],
            send_sem=e_send.at[peer],
            recv_sem=e_recv.at[at],
            device_id={"nodes": peer},
            device_id_type=MESH,
        )

    def picked(i):
        table = kvx[blocks_here : 2 * blocks_here].reshape(rows, 2 * HEAD)
        got = jnp.dot(pick[i], table, preferred_element_type=F32)
        return got.astype(BF16).reshape(ROUNDS, per, 2 * HEAD)

    @pl.loop(1, parts)
    def _(d):
        peer = node_peer(d)
        snd[peer] = picked(peer)
        e_copy(peer, p).start()

    rcv[:, p] = picked(p)

    next(weight_ring)
    for copy in neighbours:
        copy.wait_recv()

    for b in range(blocks_here):
        span = slice(b * BLOCK, (b + 1) * BLOCK)
        query = qs[span]
        scores = []
        keys = []
        for j in range(NEIGH):
            at = blocks_ref[b, j] - p * blocks_here + blocks_here
            at = jnp.minimum(jnp.maximum(at, 0), 3 * blocks_here - 1)
            block = kvx[at]
            keys.append(block)
            scores.append(lax.dot_general(query, block, NT, preferred_element_type=F32))
        top = functools.reduce(jnp.maximum, scores)
        top = jnp.max(top, axis=1, keepdims=True)
        total = jnp.zeros((BLOCK, 1), F32)
        blended = jnp.zeros((BLOCK, 2 * HEAD), F32)
        for j in range(NEIGH):
            weights = jnp.exp(scores[j] - top)
            total += jnp.sum(weights, axis=1, keepdims=True)
            blended += jnp.dot(weights.astype(BF16), keys[j], preferred_element_type=F32)
        oloc[span] = blended
        mloc[span] = jnp.broadcast_to(top, (BLOCK, 2 * HEAD))
        lloc[span] = jnp.broadcast_to(total, (BLOCK, 2 * HEAD))
        next(weight_ring, None)
    for _ in weight_ring:
        pass

    @pl.loop(1, parts)
    def _(d):
        peer = node_peer(d)
        e_copy(peer, peer).wait_recv()

    chunks = rows // 128
    for r in range(ROUNDS):
        table = rcv[r].reshape(rows, 2 * HEAD)

        @pl.loop(0, chunks)
        def _(c):
            got = jnp.dot(place[r * chunks + c], table, preferred_element_type=F32)
            far[r, pl.ds(pl.multiple_of(c * 128, 128), 128)] = got

    for b in range(blocks_here):
        span = slice(b * BLOCK, (b + 1) * BLOCK)
        query = qs[span].astype(F32)
        top = mloc[span]
        edges = []
        for r in range(ROUNDS):
            score = jnp.sum(query * far[r, span], axis=1, keepdims=True) + bias_ref[r, 0]
            edges.append(jnp.broadcast_to(score, (BLOCK, 2 * HEAD)))
        new_top = functools.reduce(jnp.maximum, edges, top)
        keep = jnp.exp(top - new_top)
        total = lloc[span] * keep
        blended = oloc[span] * keep
        for r in range(ROUNDS):
            weight = jnp.exp(edges[r] - new_top)
            total += weight
            blended += weight.astype(BF16).astype(F32) * far[r, span]
        att[span] = blended / total

    def a_copy(peer, at):
        return pltpu.make_async_remote_copy(
            src_ref=atts.at[peer],
            dst_ref=attr.at[at],
            send_sem=a_send.at[peer],
            recv_sem=a_recv.at[at],
            device_id={"tensor": peer},
            device_id_type=MESH,
        )

    left = iota((half, 2 * HEAD), 1) < HEAD

    def packed(peer):
        block = att[pl.ds(pl.multiple_of(peer * own, own), own)]
        return jnp.where(left, pltpu.roll(block[:half], HEAD, 1), block[half:]).astype(BF16)

    @pl.loop(1, peers)
    def _(d):
        peer = tensor_peer(d)
        atts[peer] = packed(peer)
        a_copy(peer, t).start()

    attr[t] = packed(t)

    @pl.loop(1, peers)
    def _(d):
        c_copy(tensor_peer(d), other_half).wait_recv()

    @pl.loop(1, peers)
    def _(d):
        peer = tensor_peer(d)
        a_copy(peer, peer).wait_recv()

    tops, bottoms = [], []
    for pair in range(peers // 2):
        even = attr[2 * pair].astype(F32)
        odd = attr[2 * pair + 1].astype(F32)
        tops.append(jnp.where(left, even, pltpu.roll(odd, HEAD, 1)).astype(BF16))
        bottoms.append(jnp.where(left, pltpu.roll(even, HEAD, 1), odd).astype(BF16))
    attended = jnp.concatenate(
        [jnp.concatenate(tops, axis=1), jnp.concatenate(bottoms, axis=1)], axis=0
    )
    result = jnp.dot(attended, woutg[...].reshape(peers * own, D), preferred_element_type=F32)
    out_ref[...] = (x_ref[...].astype(F32) + result).astype(BF16)

    @pl.loop(1, parts)
    def _(d):
        peer = node_peer(d)
        r_copy(peer, p).wait_send()
        e_copy(peer, p).wait_send()

    @pl.loop(1, peers)
    def _(d):
        peer = tensor_peer(d)
        a_copy(peer, t).wait_send()
        c_copy(peer, own_half).wait_send()

    for copy in neighbours:
        copy.wait_send()


def per_device(
    node_states,
    norm_gain,
    input_weight,
    output_weight,
    expander_bias,
    local_blocks,
    expander_source,
):
    parts = lax.axis_size("nodes")
    peers = lax.axis_size("tensor")
    own = node_states.shape[0]
    rows = own * peers
    per = rows // parts
    chunks = rows // 128
    wide = 2 * HEAD
    vmem = pl.BlockSpec(memory_space=pltpu.VMEM)
    smem = pl.BlockSpec(memory_space=pltpu.SMEM)
    dma = pltpu.SemaphoreType.DMA
    return pl.pallas_call(
        functools.partial(kernel, parts, peers),
        out_shape=jax.ShapeDtypeStruct((own, D), BF16),
        in_specs=[vmem, vmem, vmem, vmem, smem, smem, vmem],
        out_specs=vmem,
        scratch_shapes=[
            pltpu.VMEM((peers, own, D), BF16),
            pltpu.VMEM((3 * rows // BLOCK, BLOCK, wide), BF16),
            pltpu.VMEM((rows, wide), BF16),
            pltpu.VMEM((parts, 1, ROUNDS * per), F32),
            pltpu.VMEM((parts, 1, ROUNDS * per), F32),
            pltpu.VMEM((ROUNDS * chunks, 1, 128), F32),
            pltpu.VMEM((parts, ROUNDS * per, rows), BF16),
            pltpu.VMEM((ROUNDS * chunks, 128, rows), BF16),
            pltpu.VMEM((parts, ROUNDS, per, wide), BF16),
            pltpu.VMEM((ROUNDS, parts, per, wide), BF16),
            pltpu.VMEM((ROUNDS, rows, wide), F32),
            pltpu.VMEM((rows, wide), F32),
            pltpu.VMEM((rows, wide), F32),
            pltpu.VMEM((rows, wide), F32),
            pltpu.VMEM((rows, wide), F32),
            pltpu.VMEM((peers, own // 2, wide), BF16),
            pltpu.VMEM((peers, own // 2, wide), BF16),
            pltpu.VMEM((peers, own, D), BF16),
            dma((peers,)),
            dma((peers,)),
            dma((peers,)),
            dma((peers,)),
            dma((peers,)),
            dma((peers,)),
            dma((parts,)),
            dma((parts,)),
            dma((parts,)),
            dma((parts,)),
            dma((2,)),
            dma((2,)),
            dma((peers,)),
            dma((peers,)),
        ],
        compiler_params=pltpu.CompilerParams(
            collective_id=0, has_side_effects=True, vmem_limit_bytes=48 * 1024 * 1024
        ),
        cost_estimate=pl.CostEstimate(
            flops=2 * rows * D * 8 * HEAD, bytes_accessed=4 * own * D * 8, transcendentals=rows * rows
        ),
    )(
        node_states,
        norm_gain.reshape(1, D),
        input_weight,
        output_weight,
        expander_bias,
        local_blocks,
        expander_source,
    )


def solution(mesh):
    in_specs = (
        P(("nodes", "tensor"), None),
        P(),
        P("tensor", None),
        P("tensor", None),
        P(None, "tensor"),
        P("nodes", None),
        P(None, "nodes"),
    )
    out_specs = P(("nodes", "tensor"), None)
    return jax.shard_map(
        per_device, mesh=mesh, in_specs=in_specs, out_specs=out_specs, check_vma=False
    )
```

time: 289 us -> 93.4 us (0.32)
  local copies, waits for them, and re-layouts: 101 us -> 5.62 us
  Pallas kernels: 0 us -> 86.6 us
  starting transfers between devices: 62.9 us -> 0 us
  waiting for transfers between devices: 60.1 us -> 0 us
  matrix products: 16.6 us -> 0 us
  blocking collectives: 15.5 us -> 0 us
  between operations: 15.2 us -> 0.02 us
  other arithmetic: 13 us -> 0 us
    pallas_call x0 -> x1, Pallas kernels: none -> 86.6 us  [per_device(): pl.pallas_call(functools.partial(kernel, parts, peers), out_shape=jax.Sha...]
    gather x7 -> x0, local copies, waits for them, and re-layouts: 73.7 us -> none  [the longest x2 34.9 us: per_device(): jnp.take_along_axis(within, order, axis=1)]
    all_to_all x8 -> x0, starting transfers between devices: 57.3 us -> none  [the longest x4 33.1 us: per_device(): lax.all_to_all(wanted[round_index:round_index + 1], 'nodes', split_axis=1...]
    all_to_all x8 -> x0, waiting for transfers between devices: 40.5 us -> none  [the longest x4 23.7 us: per_device(): lax.all_to_all(key_values[lax.all_to_all(wanted[round_index:round_index +...]
    all_gather x2 -> x0, waiting for transfers between devices: 18.6 us -> none  [the longest x1 18.5 us: per_device(): lax.all_gather(node_states, 'tensor', axis=0, tiled=True)]
    dot_general x10 -> x0, matrix products: 16.6 us -> none  [the longest x2 4.59 us: attend_group(): jnp.einsum('bqhe,rbqhe->bhqr', group_queries, group_far, preferred_elemen...]
    all_to_all x1 -> x0, blocking collectives: 15.5 us -> none  [per_device(): lax.all_to_all(head_outputs, 'tensor', split_axis=0, concat_axis=1, tiled...]
    dynamic_slice x6 -> x0, local copies, waits for them, and re-layouts: 6.08 us -> none  [the longest x2 2.52 us: per_device(): lax.map(attend_group, jnp.arange(blocks_here // 2, dtype=jnp.int32))]
  transfers between devices with their start and end apart: 12 -> 0, of which waited for: 8 -> 0; matrix products, arithmetic and copies ran while one was open for 42% -> 0% of each run, Pallas kernels for 0% -> 0%
where the time goes in v1:
time: 93.4 us; the launch traced here: 92.2 us
  Pallas kernels  86.6 us (93%)
  local copies, waits for them, and re-layouts  5.62 us (6%)
    pallas_call x1, Pallas kernels, per_device(): pl.pallas_call(functools.partial(kernel, parts, peers), out_shape=jax.Sha...  86.6 us
    unnamed x14, local copies, waits for them, and re-layouts  5.62 us

profile of v1, /device:TPU:1, one launch (start us, length us, event | category | flops | bytes accessed | tf_op | source)
XLA Modules:
  0.0 92.2 jit_solution(17909269271677817899)
XLA Ops:
  0.0 0.0 copy-start.4
  0.0 0.8 copy.8.bias_ref
  0.8 0.0 copy-done.4
  0.8 0.0 copy-start
  0.8 1.0 %copy-done = bf16[192,1024]{1,0:T(8,128)(2,1)S(1)} copy-done((bf16[192,1024]{1,0:T(8,128)(2,1)S(1)}, bf16[192,1024]{1,0:T(8,128)(2,1)}, u32[]{:S(2)}) %copy-start) | copy-done | bytes 393240
  1.8 0.0 copy-start.1
  1.8 0.9 copy-done.1
  2.7 0.0 copy-start.2
  2.7 0.9 copy-done.2
  3.6 0.0 copy-start.3
  3.6 0.7 copy-done.3
  4.3 0.0 copy-start.5
  4.3 0.7 copy-done.5
  5.0 86.6 %shard_map.73 = bf16[64,1024]{1,0:T(8,128)(2,1)S(1)} custom-call(bf16[64,1024]{1,0:T(8,128)(2,1)S(1)} %copy-done.1, f32[1,1024]{1,0:T(1,128)S(1)} %bitcast.1, bf16[192,1024]{1,0:T(8,128)(2,1)S(1)} %copy-done, bf16[64,1024]{1,0:T(8,128)(2,1)S(1)} %copy-done.2, f32[4,1]{1,0:T(4,128)S(1)} %copy.8.bias_ref, s32[4,4]{1,0:T(4,128)S(1)} %copy-done.5, ...), custom_call_target="tpu_custom_call" | custom-call | flops 1073741824 | bytes 2097152 | tf_op jit(solution)/shard_map/pallas_call | solution.py:479
  91.5 0.7 copy.10
Async XLA Ops:
  0.0 0.8 copy-start.4
  0.8 1.0 %copy-start = (bf16[192,1024]{1,0:T(8,128)(2,1)S(1)}, bf16[192,1024]{1,0:T(8,128)(2,1)}, u32[]{:S(2)}) copy-start(bf16[192,1024]{1,0:T(8,128)(2,1)} %win_ref.1) | copy-start | bytes 1179652
  1.8 0.9 copy-start.1
  2.7 0.9 copy-start.2
  3.6 0.7 copy-start.3
  4.3 0.7 copy-start.5

commit v2 on v1

v2 whole, which is shorter than its diff:
```python
import functools
import math

import jax
import jax.numpy as jnp
from jax import lax
from jax.experimental import pallas as pl
from jax.experimental.pallas import tpu as pltpu
from jax.sharding import PartitionSpec as P

D = 1024
HEAD = 64
BLOCK = 256
NEIGH = 4
ROUNDS = 4
EPS = 1e-05
CHUNKS = 2
GROUPS = ((0, 16), (16, 24), (24, 32))

BF16 = jnp.bfloat16
F32 = jnp.float32
I32 = jnp.int32
MESH = pl.DeviceIdType.MESH
NT = (((1,), (1,)), ((), ()))


def iota(shape, dim):
    return lax.broadcasted_iota(I32, shape, dim)


def kernel(
    parts,
    peers,
    x_ref,
    gain_ref,
    win_ref,
    wout_ref,
    bias_ref,
    blocks_ref,
    src_ref,
    out_ref,
    xown,
    gain_v,
    win_v,
    win_t,
    bias_in,
    bias_out,
    bias_v,
    blocks_in,
    blocks_out,
    blocks_v,
    blocks_s,
    src_v,
    xg,
    kvx,
    qs,
    reqs,
    reqr,
    posr,
    place,
    snd,
    rcv,
    far,
    oloc,
    mloc,
    lloc,
    att,
    atts,
    attr,
    woutg,
    l_sem,
    s_sem,
    g_sem,
    x_send,
    x_recv,
    h_send,
    h_recv,
    w_send,
    w_recv,
    c_send,
    c_recv,
    r_send,
    r_recv,
    e_send,
    e_recv,
    n_send,
    n_recv,
    a_send,
    a_recv,
):
    own = x_ref.shape[0]
    rows = own * peers
    ring = peers // 2
    per = rows // parts
    blocks_here = rows // BLOCK
    wide = 2 * HEAD
    row_chunks = rows // 128
    p = lax.axis_index("nodes")
    t = lax.axis_index("tensor")
    core = p % 2
    base = p - core
    y, xh = t // 2, t % 2
    part = base + xh
    head = 2 * y + core
    home = core == xh

    def device(nodes, tensor):
        return {"nodes": nodes, "tensor": tensor}

    def worker(partition):
        return device(partition - partition % 2 + core, y * 2 + partition % 2)

    def distance(i):
        q, a = i // 2, i % 2
        return 8 + 16 * a + (q // 2) * (1 - q % 2) - ((q + 1) // 2) * (q % 2)

    def ahead(i):
        return worker((part + distance(i)) % parts)

    def behind(i):
        return worker((part + parts - distance(i)) % parts)

    self_slot = parts - 2
    up = device(p, ((y + 1) % ring) * 2 + xh)
    down = device(p, ((y + ring - 1) % ring) * 2 + xh)
    twin = device(base + 1 - core, t)
    swap = device(base + 1 - core, y * 2 + 1 - xh)
    cross = device((base + parts // 2) % parts + 1 - core, y * 2 + 1 - xh)
    across = device((p + parts // 2) % parts, y * 2 + 1 - xh)

    x_in = pltpu.make_async_copy(x_ref, xown, l_sem.at[0])
    gain_in = pltpu.make_async_copy(gain_ref, gain_v, l_sem.at[1])
    bias_load = pltpu.make_async_copy(bias_ref, bias_in, l_sem.at[2])
    blocks_load = pltpu.make_async_copy(blocks_ref, blocks_in, l_sem.at[3])
    wout_in = pltpu.make_async_copy(wout_ref, woutg.at[t], l_sem.at[4])
    for copy in (bias_load, blocks_load, gain_in, x_in, wout_in):
        copy.start()

    def local(source, target, sem):
        return pltpu.make_async_copy(source, target, sem)

    def remote(source, target, send, recv, to):
        return pltpu.make_async_remote_copy(
            src_ref=source,
            dst_ref=target,
            send_sem=send,
            recv_sem=recv,
            device_id=to,
            device_id_type=MESH,
        )

    chunk = own // CHUNKS

    def piece(at, c):
        return xg.at[at, pl.ds(c * chunk, chunk)]

    @pl.when(home)
    def _():
        for c in range(CHUNKS):
            local(x_ref.at[pl.ds(c * chunk, chunk)], piece(t, c), x_recv.at[t, c]).start()
        local(win_ref, win_v, g_sem.at[0]).start()
        local(src_ref, src_v, g_sem.at[1]).start()

    barrier = pltpu.get_barrier_semaphore()

    def greet(to):
        pl.semaphore_signal(barrier, inc=1, device_id=to, device_id_type=MESH)

    for to in (up, down, twin, swap, cross):
        greet(to)

    @pl.loop(0, parts)
    def _(i):
        @pl.when(i != self_slot)
        def _():
            greet(ahead(i))

    bias_load.wait()
    bias_out[...] = jnp.broadcast_to(
        jnp.concatenate([bias_in[...], jnp.zeros((8 - ROUNDS, 1), F32)], axis=0), (8, 128)
    )
    blocks_load.wait()
    blocks_out[0:blocks_here, 0:NEIGH] = blocks_in[...]

    @pl.when(home)
    def _():
        bias_v[...] = bias_out[...]
        blocks_v[...] = blocks_out[...]

    pl.semaphore_wait(barrier, parts + 4)

    def swap_x(c):
        return remote(
            x_ref.at[pl.ds(c * chunk, chunk)], piece(t, c), s_sem.at[c], x_recv.at[t, c], swap
        )

    cross_w = remote(win_ref, win_v, s_sem.at[CHUNKS], g_sem.at[0], cross)
    cross_b = remote(bias_out, bias_v, s_sem.at[CHUNKS + 1], g_sem.at[2], cross)
    twin_s = remote(src_ref, src_v, s_sem.at[0], g_sem.at[1], twin)
    twin_b = remote(blocks_out, blocks_v, s_sem.at[1], g_sem.at[3], twin)

    @pl.when(jnp.logical_not(home))
    def _():
        for c in range(CHUNKS):
            swap_x(c).start()
        cross_w.start()
        cross_b.start()

    @pl.when(home)
    def _():
        twin_s.start()
        twin_b.start()

    sent = []

    def x_forward(at, c, to):
        copy = remote(piece(at, c), piece(at, c), x_send.at[len(sent)], x_recv.at[at, c], to)
        copy.start()
        sent.append(copy)

    def x_wait(at, c):
        remote(piece(at, c), piece(at, c), x_send.at[0], x_recv.at[at, c], up).wait_recv()

    def hand(at):
        return remote(xg.at[at], xg.at[at], h_send.at[at // 2], h_recv.at[at // 2], twin)

    def mate(k):
        return (y + ring + k) % ring

    first = 2 * y + core
    for c in range(CHUNKS):
        x_wait(first, c)
        x_forward(first, c, up)
        x_forward(first, c, down)
    hand(first).start()

    local(src_ref, src_v, g_sem.at[1]).wait()
    src = src_v[...]
    owner = lax.shift_right_logical(src, rows.bit_length() - 1)
    within = (src & (rows - 1)).astype(F32)
    gap = (part + parts - owner) & (parts - 1)
    offset = (gap & (parts // 2 - 1)) - parts // 4
    turn = jnp.where(offset < 0, -2 * offset - 1, 2 * offset)
    slot = 2 * turn + lax.shift_right_logical(gap, (parts // 2).bit_length() - 1)
    high = jnp.floor(within * (1.0 / per))
    low = within - high * per
    slot_rows = iota((parts, rows), 0)
    belongs = [slot[r : r + 1] == slot_rows for r in range(ROUNDS)]
    before = jnp.where(iota((rows, rows), 0) < iota((rows, rows), 1), 1.0, 0.0).astype(BF16)
    member = jnp.concatenate([jnp.where(b, 1.0, 0.0) for b in belongs], axis=0).astype(BF16)
    counts = jnp.dot(member, before, preferred_element_type=F32)
    entry = iota((ROUNDS * per, rows), 0).astype(F32)
    wanted_high = jnp.zeros((parts, ROUNDS * per), F32)
    wanted_low = jnp.zeros((parts, ROUNDS * per), F32)
    for r in range(ROUNDS):
        rank = jnp.sum(
            jnp.where(belongs[r], counts[r * parts : (r + 1) * parts], 0.0), axis=0, keepdims=True
        )
        position = slot[r : r + 1].astype(F32) * per + rank
        for c in range(row_chunks):
            posr[r * row_chunks + c] = position[:, c * 128 : (c + 1) * 128]
        chosen = jnp.where(entry == rank + r * per, 1.0, 0.0).astype(BF16)
        wanted_high += lax.dot_general(
            jnp.where(belongs[r], high[r : r + 1], 0.0).astype(BF16),
            chosen,
            NT,
            preferred_element_type=F32,
        )
        wanted_low += lax.dot_general(
            jnp.where(belongs[r], low[r : r + 1], 0.0).astype(BF16),
            chosen,
            NT,
            preferred_element_type=F32,
        )
    wanted = wanted_high * per + wanted_low
    for i in range(parts):
        reqs[i] = wanted[i : i + 1]

    def r_copy(i, to):
        return remote(reqs.at[i], reqr.at[i], r_send.at[i], r_recv.at[i], to)

    @pl.loop(0, parts)
    def _(i):
        @pl.when(i != self_slot)
        def _():
            r_copy(i, behind(i)).start()

    reqr[self_slot] = reqs[self_slot]

    local(win_ref, win_v, g_sem.at[0]).wait()
    win_t[...] = jnp.transpose(win_v[...].astype(F32)).astype(BF16)
    gain_in.wait()
    gain = gain_v[...]
    wide_lane = iota((2 * own, wide), 1)

    def project(pair):
        hand(2 * pair + 1 - core).wait_recv()
        states = xg[pl.ds(2 * pair, 2)].reshape(2 * own, D).astype(F32)
        inverse = lax.rsqrt(jnp.sum(states * states, axis=1, keepdims=True) / D + EPS)
        scaled = (states * gain).astype(BF16)
        totals = jnp.dot(scaled, win_t[...], preferred_element_type=F32) * inverse
        start = pl.multiple_of(pair * 2 * own, 2 * own)
        query = totals[:, :wide].astype(BF16).astype(F32) * (1.0 / math.sqrt(HEAD))
        qs[pl.ds(start, 2 * own)] = jnp.where(wide_lane < HEAD, query, 0.0).astype(BF16)
        pairs = BLOCK // (2 * own)
        inside = pl.multiple_of(pair % pairs * 2 * own, 2 * own)
        kvx[blocks_here + pair // pairs, pl.ds(inside, 2 * own)] = totals[:, HEAD:].astype(BF16)

    last = ring // 2
    for k in range(1, last):
        below, above = 2 * mate(-k) + core, 2 * mate(k) + core
        for c in range(CHUNKS):
            x_wait(below, c)
            if k < last - 1 or c < CHUNKS // 2:
                x_forward(below, c, up)
            x_wait(above, c)
            if k < last - 1 or c >= CHUNKS // 2:
                x_forward(above, c, down)
        hand(below).start()
        hand(above).start()
        if k == 1:
            project(y)
        else:
            project(mate(1 - k))
            project(mate(k - 1))
    opposite = 2 * mate(last) + core
    for c in range(CHUNKS):
        x_wait(opposite, c)
    hand(opposite).start()
    project(mate(1 - last))
    project(mate(last - 1))
    project(mate(last))

    mine = kvx.at[pl.ds(blocks_here, blocks_here)]
    neighbours = [
        remote(
            mine,
            kvx.at[pl.ds(2 * blocks_here * which, blocks_here)],
            n_send.at[which],
            n_recv.at[which],
            to,
        )
        for which, to in enumerate((worker((part + 1) % parts), worker((part + parts - 1) % parts)))
    ]

    half = own // 2
    own_half = pl.ds(pl.multiple_of(core * half, half), half)
    other_half = pl.ds(pl.multiple_of((1 - core) * half, half), half)
    weights_sent = []

    def w_send_to(source, at, to):
        copy = remote(
            source, woutg.at[at, own_half], w_send.at[len(weights_sent)], w_recv.at[at], to
        )
        copy.start()
        weights_sent.append(copy)

    def w_wait(at):
        part_of = woutg.at[at, own_half]
        remote(part_of, part_of, w_send.at[0], w_recv.at[at], up).wait_recv()

    def c_copy(at, side):
        part_of = woutg.at[at, side]
        return remote(part_of, part_of, c_send.at[at], c_recv.at[at], twin)

    def weight_ring():
        mine = wout_ref.at[own_half]
        for to in (up, down, across):
            w_send_to(mine, t, to)
        yield
        at = 2 * y + 1 - xh
        w_wait(at)
        for to in (up, down):
            w_send_to(woutg.at[at, own_half], at, to)
        c_copy(at, own_half).start()
        yield
        for k in range(1, last + 1):
            for column in range(2):
                side = xh if column == 0 else 1 - xh
                for way, to in ((-k, up), (k, down)):
                    turned = column == 0 if way < 0 else column == 1
                    if k == last and not turned:
                        continue
                    at = 2 * mate(way) + side
                    w_wait(at)
                    if k < last - 1 or (k == last - 1 and turned):
                        w_send_to(woutg.at[at, own_half], at, to)
                    c_copy(at, own_half).start()
            yield

    weight_steps = weight_ring()

    diagonal = iota((128, 128), 0) == iota((128, 128), 1)
    lane_index = iota((128, rows), 1).astype(F32)

    def one_hot(row):
        column = jnp.sum(jnp.where(diagonal, row, 0.0), axis=1, keepdims=True)
        return jnp.where(lane_index == column, 1.0, 0.0).astype(BF16)

    def e_copy(i, to):
        return remote(snd.at[i], rcv.at[:, i], e_send.at[i], e_recv.at[i], to)

    def picked(i):
        table = kvx[blocks_here : 2 * blocks_here].reshape(rows, wide)
        got = jnp.dot(one_hot(reqr[i]), table, preferred_element_type=F32)
        return got.astype(BF16).reshape(ROUNDS, per, wide)

    steps = 4
    for step in range(steps):

        @pl.loop(step * parts // steps, (step + 1) * parts // steps)
        def _(i):
            @pl.when(i != self_slot)
            def _():
                r_copy(i, ahead(i)).wait_recv()
                snd[i] = picked(i)
                e_copy(i, ahead(i)).start()

        if step == 0:
            for copy in neighbours:
                copy.start()
        next(weight_steps)

    rcv[:, self_slot] = picked(self_slot)

    @pl.loop(0, ROUNDS * row_chunks)
    def _(i):
        place[i] = one_hot(posr[i])

    for _ in weight_steps:
        pass

    @pl.when(jnp.logical_not(home))
    def _():
        cross_b.wait_recv()
        twin_b.wait_recv()

    blocks_copy = pltpu.make_async_copy(blocks_v, blocks_s, l_sem.at[3])
    blocks_copy.start()
    blocks_copy.wait()
    for copy in neighbours:
        copy.wait_recv()
    for b in range(blocks_here):
        span = slice(b * BLOCK, (b + 1) * BLOCK)
        query = qs[span]
        scores = []
        keys = []
        for j in range(NEIGH):
            at = blocks_s[b, j] - part * blocks_here + blocks_here
            at = jnp.minimum(jnp.maximum(at, 0), 3 * blocks_here - 1)
            block = kvx[at]
            keys.append(block)
            scores.append(lax.dot_general(query, block, NT, preferred_element_type=F32))
        top = functools.reduce(jnp.maximum, scores)
        top = jnp.max(top, axis=1, keepdims=True)
        total = jnp.zeros((BLOCK, 1), F32)
        blended = jnp.zeros((BLOCK, wide), F32)
        for j in range(NEIGH):
            weights = jnp.exp(scores[j] - top)
            total += jnp.sum(weights, axis=1, keepdims=True)
            blended += jnp.dot(weights.astype(BF16), keys[j], preferred_element_type=F32)
        oloc[span] = blended
        mloc[span] = jnp.broadcast_to(top, (BLOCK, wide))
        lloc[span] = jnp.broadcast_to(total, (BLOCK, wide))

    for group, (low_slot, high_slot) in enumerate(GROUPS):

        @pl.loop(low_slot, high_slot)
        def _(i):
            @pl.when(i != self_slot)
            def _():
                e_copy(i, behind(i)).wait_recv()

        for r in range(ROUNDS):
            table = rcv[r, low_slot:high_slot].reshape((high_slot - low_slot) * per, wide)

            @pl.loop(0, row_chunks)
            def _(c):
                chosen = place[r * row_chunks + c, :, low_slot * per : high_slot * per]
                got = jnp.dot(chosen, table, preferred_element_type=F32)
                span = pl.ds(pl.multiple_of(c * 128, 128), 128)
                if group == 0:
                    far[r, span] = got
                else:
                    far[r, span] += got

    for b in range(blocks_here):
        span = slice(b * BLOCK, (b + 1) * BLOCK)
        query = qs[span].astype(F32)
        top = mloc[span]
        edges = []
        for r in range(ROUNDS):
            score = jnp.sum(query * far[r, span], axis=1, keepdims=True)
            edges.append(jnp.broadcast_to(score, (BLOCK, wide)) + bias_v[r : r + 1])
        new_top = functools.reduce(jnp.maximum, edges, top)
        keep = jnp.exp(top - new_top)
        total = lloc[span] * keep
        blended = oloc[span] * keep
        for r in range(ROUNDS):
            weight = jnp.exp(edges[r] - new_top)
            total += weight
            blended += weight.astype(BF16).astype(F32) * far[r, span]
        att[span] = blended / total

    left = iota((half, wide), 1) < HEAD

    def packed(at):
        block = att[pl.ds(pl.multiple_of(at * own, own), own)]
        return jnp.where(left, pltpu.roll(block[:half], HEAD, 1), block[half:]).astype(BF16)

    def a_copy(source, to_at, slot_at, send):
        return remote(
            source, attr.at[slot_at], a_send.at[send], a_recv.at[slot_at], device(part, to_at)
        )

    order = [(k, s) for k in (4, 3, -3, 2, -2, 1, -1, 0) for s in (1, 0)]
    owners = [2 * mate(k) + ((xh + s) % 2) for k, s in order]
    for i, at in enumerate(owners):
        if i < len(owners) - 1:
            atts[i] = packed(at)
            a_copy(atts.at[i], at, head, i).start()
        else:
            atts[i] = packed(at)

            @pl.when(home)
            def _():
                attr[head] = atts[i]

            @pl.when(jnp.logical_not(home))
            def _():
                a_copy(atts.at[i], at, head, i).start()

    for at in range(peers):

        @pl.when(at != t)
        def _():
            c_copy(at, other_half).wait_recv()

    wout_in.wait()
    x_in.wait()
    for at in range(peers):

        @pl.when(jnp.logical_or(at != head, jnp.logical_not(home)))
        def _():
            a_copy(atts.at[0], t, at, 0).wait_recv()

    tops, bottoms = [], []
    for pair in range(peers // 2):
        even = attr[2 * pair].astype(F32)
        odd = attr[2 * pair + 1].astype(F32)
        tops.append(jnp.where(left, even, pltpu.roll(odd, HEAD, 1)).astype(BF16))
        bottoms.append(jnp.where(left, pltpu.roll(even, HEAD, 1), odd).astype(BF16))
    attended = jnp.concatenate(
        [jnp.concatenate(tops, axis=1), jnp.concatenate(bottoms, axis=1)], axis=0
    )
    result = jnp.dot(attended, woutg[...].reshape(peers * own, D), preferred_element_type=F32)
    out_ref[...] = (xown[...].astype(F32) + result).astype(BF16)

    @pl.when(jnp.logical_not(home))
    def _():
        for c in range(CHUNKS):
            swap_x(c).wait_send()
        cross_w.wait_send()
        cross_b.wait_send()
        a_copy(atts.at[peers - 1], owners[-1], head, peers - 1).wait_send()

    @pl.when(home)
    def _():
        twin_s.wait_send()
        twin_b.wait_send()

    for copy in sent + weights_sent + neighbours:
        copy.wait_send()

    @pl.loop(0, parts)
    def _(i):
        @pl.when(i != self_slot)
        def _():
            r_copy(i, behind(i)).wait_send()
            e_copy(i, ahead(i)).wait_send()

    for k in range(ring):
        hand(2 * k + core).wait_send()
    for i in range(peers - 1):
        a_copy(atts.at[i], owners[i], head, i).wait_send()
    for at in range(peers):

        @pl.when(at != t)
        def _():
            c_copy(at, own_half).wait_send()


def per_device(
    node_states,
    norm_gain,
    input_weight,
    output_weight,
    expander_bias,
    local_blocks,
    expander_source,
):
    parts = lax.axis_size("nodes")
    peers = lax.axis_size("tensor")
    own = node_states.shape[0]
    rows = own * peers
    per = rows // parts
    chunks = rows // 128
    wide = 2 * HEAD
    blocks_here = rows // BLOCK
    dma = pltpu.SemaphoreType.DMA
    vmem = pltpu.VMEM
    return pl.pallas_call(
        functools.partial(kernel, parts, peers),
        out_shape=jax.ShapeDtypeStruct((own, D), BF16),
        in_specs=[pl.BlockSpec(memory_space=pl.ANY)] * 7,
        out_specs=pl.BlockSpec(memory_space=pltpu.VMEM),
        scratch_shapes=[
            vmem((own, D), BF16),
            vmem((1, D), F32),
            vmem((3 * HEAD, D), BF16),
            vmem((D, 3 * HEAD), BF16),
            vmem((ROUNDS, 1), F32),
            vmem((8, 128), F32),
            vmem((8, 128), F32),
            vmem((blocks_here, NEIGH), I32),
            vmem((8, 128), I32),
            vmem((8, 128), I32),
            pltpu.SMEM((8, 128), I32),
            vmem((ROUNDS, rows), I32),
            vmem((peers, own, D), BF16),
            vmem((3 * blocks_here, BLOCK, wide), BF16),
            vmem((rows, wide), BF16),
            vmem((parts, 1, ROUNDS * per), F32),
            vmem((parts, 1, ROUNDS * per), F32),
            vmem((ROUNDS * chunks, 1, 128), F32),
            vmem((ROUNDS * chunks, 128, rows), BF16),
            vmem((parts, ROUNDS, per, wide), BF16),
            vmem((ROUNDS, parts, per, wide), BF16),
            vmem((ROUNDS, rows, wide), F32),
            vmem((rows, wide), F32),
            vmem((rows, wide), F32),
            vmem((rows, wide), F32),
            vmem((rows, wide), F32),
            vmem((peers, own // 2, wide), BF16),
            vmem((peers, own // 2, wide), BF16),
            vmem((peers, own, D), BF16),
            dma((5,)),
            dma((CHUNKS + 2,)),
            dma((4,)),
            dma((8 * CHUNKS,)),
            dma((peers, CHUNKS)),
            dma((peers // 2,)),
            dma((peers // 2,)),
            dma((peers,)),
            dma((peers,)),
            dma((peers,)),
            dma((peers,)),
            dma((parts,)),
            dma((parts,)),
            dma((parts,)),
            dma((parts,)),
            dma((2,)),
            dma((2,)),
            dma((peers,)),
            dma((peers,)),
        ],
        compiler_params=pltpu.CompilerParams(
            collective_id=0, has_side_effects=True, vmem_limit_bytes=40 * 1024 * 1024
        ),
        cost_estimate=pl.CostEstimate(
            flops=2 * rows * D * 8 * HEAD, bytes_accessed=4 * own * D * 8, transcendentals=rows * rows
        ),
    )(
        node_states,
        norm_gain.reshape(1, D),
        input_weight,
        output_weight,
        expander_bias,
        local_blocks,
        expander_source,
    )


def solution(mesh):
    in_specs = (
        P(("nodes", "tensor"), None),
        P(),
        P("tensor", None),
        P("tensor", None),
        P(None, "tensor"),
        P("nodes", None),
        P(None, "nodes"),
    )
    out_specs = P(("nodes", "tensor"), None)
    return jax.shard_map(
        per_device, mesh=mesh, in_specs=in_specs, out_specs=out_specs, check_vma=False
    )
```

time: 93.4 us -> 113 us (1.21)
  the two profiles are of different devices: /device:TPU:1 before, /device:TPU:4 now
where the time goes in v2:
time: 113 us; the launch traced here: 112 us
  Pallas kernels  107 us (95%)
  local copies, waits for them, and re-layouts  5.62 us (5%)
    pallas_call x1, Pallas kernels, per_device(): pl.pallas_call(functools.partial(kernel, parts, peers), out_shape=jax.Sha...  107 us
    unnamed x14, local copies, waits for them, and re-layouts  5.62 us

profile of v2, /device:TPU:4, one launch (start us, length us, event | category | flops | bytes accessed | tf_op | source)
XLA Modules:
  0.0 112.4 jit_solution(9302996426944869753)
XLA Ops:
  0.0 0.0 copy-start.4
  0.0 0.8 copy.8.bias_ref
  0.8 0.0 copy-done.4
  0.8 0.0 copy-start
  0.8 1.0 copy-done
  1.8 0.0 copy-start.1
  1.8 0.9 copy-done.1
  2.7 0.0 copy-start.2
  2.7 0.9 copy-done.2
  3.6 0.0 copy-start.3
  3.6 0.7 copy-done.3
  4.3 0.0 copy-start.5
  4.3 0.7 copy-done.5
  5.0 106.7 %shard_map.73 = bf16[64,1024]{1,0:T(8,128)(2,1)S(1)} custom-call(bf16[64,1024]{1,0:T(8,128)(2,1)S(1)} %copy-done.1, f32[1,1024]{1,0:T(1,128)S(1)} %bitcast.1, bf16[192,1024]{1,0:T(8,128)(2,1)S(1)} %copy-done, bf16[64,1024]{1,0:T(8,128)(2,1)S(1)} %copy-done.2, f32[4,1]{1,0:T(4,128)S(1)} %copy.8.bias_ref, s32[4,4]{1,0:T(4,128)S(1)} %copy-done.5, ...), custom_call_target="tpu_custom_call" | custom-call | flops 1073741824 | bytes 2097152 | tf_op jit(solution)/shard_map/pallas_call | solution.py:612
  111.7 0.7 copy.10
Async XLA Ops:
  0.0 0.8 copy-start.4
  0.8 1.0 copy-start
  1.8 0.9 copy-start.1
  2.7 0.9 copy-start.2
  3.6 0.7 copy-start.3
  4.3 0.7 copy-start.5

commit v3 on v2

--- a/solution.py
+++ b/solution.py
@@ -15,7 +15,6 @@
 ROUNDS = 4
 EPS = 1e-05
 CHUNKS = 2
-GROUPS = ((0, 16), (16, 24), (24, 32))
 
 BF16 = jnp.bfloat16
 F32 = jnp.float32
@@ -60,11 +59,9 @@
     place,
     snd,
     rcv,
-    far,
     oloc,
     mloc,
     lloc,
-    att,
     atts,
     attr,
     woutg,
@@ -125,6 +122,8 @@
     down = device(p, ((y + ring - 1) % ring) * 2 + xh)
     twin = device(base + 1 - core, t)
     swap = device(base + 1 - core, y * 2 + 1 - xh)
+    swap_up = device(base + 1 - core, ((y + 1) % ring) * 2 + 1 - xh)
+    swap_down = device(base + 1 - core, ((y + ring - 1) % ring) * 2 + 1 - xh)
     cross = device((base + parts // 2) % parts + 1 - core, y * 2 + 1 - xh)
     across = device((p + parts // 2) % parts, y * 2 + 1 - xh)
 
@@ -166,7 +165,7 @@
     def greet(to):
         pl.semaphore_signal(barrier, inc=1, device_id=to, device_id_type=MESH)
 
-    for to in (up, down, twin, swap, cross):
+    for to in (up, down, twin, swap, swap_up, swap_down, cross):
         greet(to)
 
     @pl.loop(0, parts)
@@ -176,9 +175,8 @@
             greet(ahead(i))
 
     bias_load.wait()
-    bias_out[...] = jnp.broadcast_to(
-        jnp.concatenate([bias_in[...], jnp.zeros((8 - ROUNDS, 1), F32)], axis=0), (8, 128)
-    )
+    for r in range(ROUNDS):
+        bias_out[r : r + 1] = jnp.broadcast_to(bias_in[:, r : r + 1], (1, 128))
     blocks_load.wait()
     blocks_out[0:blocks_here, 0:NEIGH] = blocks_in[...]
 
@@ -187,22 +185,27 @@
         bias_v[...] = bias_out[...]
         blocks_v[...] = blocks_out[...]
 
-    pl.semaphore_wait(barrier, parts + 4)
-
-    def swap_x(c):
+    pl.semaphore_wait(barrier, parts + 6)
+
+    def swap_x(c, to):
         return remote(
-            x_ref.at[pl.ds(c * chunk, chunk)], piece(t, c), s_sem.at[c], x_recv.at[t, c], swap
-        )
-
-    cross_w = remote(win_ref, win_v, s_sem.at[CHUNKS], g_sem.at[0], cross)
-    cross_b = remote(bias_out, bias_v, s_sem.at[CHUNKS + 1], g_sem.at[2], cross)
-    twin_s = remote(src_ref, src_v, s_sem.at[0], g_sem.at[1], twin)
-    twin_b = remote(blocks_out, blocks_v, s_sem.at[1], g_sem.at[3], twin)
+            x_ref.at[pl.ds(c * chunk, chunk)],
+            piece(t, c),
+            s_sem.at[to * CHUNKS + c],
+            x_recv.at[t, c],
+            (swap, swap_up, swap_down)[to],
+        )
+
+    cross_w = remote(win_ref, win_v, s_sem.at[3 * CHUNKS], g_sem.at[0], cross)
+    cross_b = remote(bias_out, bias_v, s_sem.at[3 * CHUNKS + 1], g_sem.at[2], cross)
+    twin_s = remote(src_ref, src_v, s_sem.at[3 * CHUNKS], g_sem.at[1], twin)
+    twin_b = remote(blocks_out, blocks_v, s_sem.at[3 * CHUNKS + 1], g_sem.at[3], twin)
 
     @pl.when(jnp.logical_not(home))
     def _():
         for c in range(CHUNKS):
-            swap_x(c).start()
+            for to in (1, 2, 0):
+                swap_x(c, to).start()
         cross_w.start()
         cross_b.start()
 
@@ -228,10 +231,21 @@
         return (y + ring + k) % ring
 
     first = 2 * y + core
+
+    def lead(c, to):
+        start = x_ref.at[pl.ds(c * chunk, chunk)]
+        return remote(
+            start, piece(t, c), s_sem.at[2 * c + to], x_recv.at[t, c], (up, down)[to]
+        )
+
+    @pl.when(home)
+    def _():
+        for c in range(CHUNKS):
+            for to in range(2):
+                lead(c, to).start()
+
     for c in range(CHUNKS):
         x_wait(first, c)
-        x_forward(first, c, up)
-        x_forward(first, c, down)
     hand(first).start()
 
     local(src_ref, src_v, g_sem.at[1]).wait()
@@ -279,32 +293,34 @@
     def r_copy(i, to):
         return remote(reqs.at[i], reqr.at[i], r_send.at[i], r_recv.at[i], to)
 
-    @pl.loop(0, parts)
-    def _(i):
-        @pl.when(i != self_slot)
-        def _():
-            r_copy(i, behind(i)).start()
-
-    reqr[self_slot] = reqs[self_slot]
-
-    local(win_ref, win_v, g_sem.at[0]).wait()
-    win_t[...] = jnp.transpose(win_v[...].astype(F32)).astype(BF16)
     gain_in.wait()
-    gain = gain_v[...]
     wide_lane = iota((2 * own, wide), 1)
+    pairs = BLOCK // (2 * own)
+    neighbours = (worker((part + 1) % parts), worker((part + parts - 1) % parts))
+
+    def n_copy(pair, which):
+        inside = pl.ds(pl.multiple_of(pair % pairs * 2 * own, 2 * own), 2 * own)
+        return remote(
+            kvx.at[blocks_here + pair // pairs, inside],
+            kvx.at[2 * blocks_here * which + pair // pairs, inside],
+            n_send.at[which, pair],
+            n_recv.at[which, pair],
+            neighbours[which],
+        )
 
     def project(pair):
         hand(2 * pair + 1 - core).wait_recv()
         states = xg[pl.ds(2 * pair, 2)].reshape(2 * own, D).astype(F32)
         inverse = lax.rsqrt(jnp.sum(states * states, axis=1, keepdims=True) / D + EPS)
-        scaled = (states * gain).astype(BF16)
+        scaled = (states * gain_v[...]).astype(BF16)
         totals = jnp.dot(scaled, win_t[...], preferred_element_type=F32) * inverse
         start = pl.multiple_of(pair * 2 * own, 2 * own)
         query = totals[:, :wide].astype(BF16).astype(F32) * (1.0 / math.sqrt(HEAD))
         qs[pl.ds(start, 2 * own)] = jnp.where(wide_lane < HEAD, query, 0.0).astype(BF16)
-        pairs = BLOCK // (2 * own)
         inside = pl.multiple_of(pair % pairs * 2 * own, 2 * own)
         kvx[blocks_here + pair // pairs, pl.ds(inside, 2 * own)] = totals[:, HEAD:].astype(BF16)
+        for which in range(2):
+            n_copy(pair, which).start()
 
     last = ring // 2
     for k in range(1, last):
@@ -319,10 +335,22 @@
         hand(below).start()
         hand(above).start()
         if k == 1:
+            @pl.loop(0, parts)
+            def _(i):
+                @pl.when(i != self_slot)
+                def _():
+                    r_copy(i, behind(i)).start()
+
+            reqr[self_slot] = reqs[self_slot]
+
+        elif k == 2:
+            local(win_ref, win_v, g_sem.at[0]).wait()
+            win_t[...] = jnp.transpose(win_v[...].astype(F32)).astype(BF16)
             project(y)
         else:
-            project(mate(1 - k))
-            project(mate(k - 1))
+            for near in range(1, k):
+                project(mate(-near))
+                project(mate(near))
     opposite = 2 * mate(last) + core
     for c in range(CHUNKS):
         x_wait(opposite, c)
@@ -330,18 +358,6 @@
     project(mate(1 - last))
     project(mate(last - 1))
     project(mate(last))
-
-    mine = kvx.at[pl.ds(blocks_here, blocks_here)]
-    neighbours = [
-        remote(
-            mine,
-            kvx.at[pl.ds(2 * blocks_here * which, blocks_here)],
-            n_send.at[which],
-            n_recv.at[which],
-            to,
-        )
-        for which, to in enumerate((worker((part + 1) % parts), worker((part + parts - 1) % parts)))
-    ]
 
     half = own // 2
     own_half = pl.ds(pl.multiple_of(core * half, half), half)
@@ -400,32 +416,46 @@
     def e_copy(i, to):
         return remote(snd.at[i], rcv.at[:, i], e_send.at[i], e_recv.at[i], to)
 
-    def picked(i):
+    batch = 4
+
+    def pick(step):
         table = kvx[blocks_here : 2 * blocks_here].reshape(rows, wide)
-        got = jnp.dot(one_hot(reqr[i]), table, preferred_element_type=F32)
-        return got.astype(BF16).reshape(ROUNDS, per, wide)
-
-    steps = 4
-    for step in range(steps):
-
-        @pl.loop(step * parts // steps, (step + 1) * parts // steps)
-        def _(i):
+        chosen = [one_hot(reqr[step * batch + j]) for j in range(batch)]
+        got = jnp.dot(jnp.concatenate(chosen, axis=0), table, preferred_element_type=F32)
+        snd[pl.ds(step * batch, batch)] = got.astype(BF16).reshape(batch, ROUNDS, per, wide)
+
+    def serve(step):
+        for j in range(batch):
+            i = step * batch + j
+
             @pl.when(i != self_slot)
             def _():
                 r_copy(i, ahead(i)).wait_recv()
-                snd[i] = picked(i)
+
+        pick(step)
+        for j in range(batch):
+            i = step * batch + j
+
+            @pl.when(i != self_slot)
+            def _():
                 e_copy(i, ahead(i)).start()
 
-        if step == 0:
-            for copy in neighbours:
-                copy.start()
+    quarters = 4
+    each = parts // batch // quarters
+    for quarter in range(quarters):
+
+        @pl.loop(quarter * each, (quarter + 1) * each)
+        def _(step):
+            serve(step)
+
         next(weight_steps)
 
-    rcv[:, self_slot] = picked(self_slot)
+    rcv[:, self_slot] = snd[self_slot]
 
     @pl.loop(0, ROUNDS * row_chunks)
     def _(i):
-        place[i] = one_hot(posr[i])
+        span = pl.ds(pl.multiple_of(i % row_chunks * 128, 128), 128)
+        place[i // row_chunks, span] = one_hot(posr[i])
 
     for _ in weight_steps:
         pass
@@ -438,8 +468,9 @@
     blocks_copy = pltpu.make_async_copy(blocks_v, blocks_s, l_sem.at[3])
     blocks_copy.start()
     blocks_copy.wait()
-    for copy in neighbours:
-        copy.wait_recv()
+    for pair in range(ring):
+        for which in range(2):
+            n_copy(pair, which).wait_recv()
     for b in range(blocks_here):
         span = slice(b * BLOCK, (b + 1) * BLOCK)
         query = qs[span]
@@ -463,34 +494,36 @@
         mloc[span] = jnp.broadcast_to(top, (BLOCK, wide))
         lloc[span] = jnp.broadcast_to(total, (BLOCK, wide))
 
-    for group, (low_slot, high_slot) in enumerate(GROUPS):
-
-        @pl.loop(low_slot, high_slot)
-        def _(i):
-            @pl.when(i != self_slot)
-            def _():
-                e_copy(i, behind(i)).wait_recv()
-
-        for r in range(ROUNDS):
-            table = rcv[r, low_slot:high_slot].reshape((high_slot - low_slot) * per, wide)
-
-            @pl.loop(0, row_chunks)
-            def _(c):
-                chosen = place[r * row_chunks + c, :, low_slot * per : high_slot * per]
-                got = jnp.dot(chosen, table, preferred_element_type=F32)
-                span = pl.ds(pl.multiple_of(c * 128, 128), 128)
-                if group == 0:
-                    far[r, span] = got
-                else:
-                    far[r, span] += got
-
-    for b in range(blocks_here):
-        span = slice(b * BLOCK, (b + 1) * BLOCK)
+    @pl.loop(0, parts)
+    def _(i):
+        @pl.when(i != self_slot)
+        def _():
+            e_copy(i, behind(i)).wait_recv()
+
+    left = iota((half, wide), 1) < HEAD
+    share = BLOCK // own
+
+    def a_copy(i, at):
+        return remote(
+            atts.at[i], attr.at[head], a_send.at[i], a_recv.at[head], device(part, at)
+        )
+
+    def a_wait(at):
+        remote(atts.at[0], attr.at[at], a_send.at[0], a_recv.at[at], up).wait_recv()
+
+    owners = []
+    for turned in (2, 1, 3, 0):
+        b = (t // share + turned) % blocks_here
+        span = pl.ds(pl.multiple_of(b * BLOCK, BLOCK), BLOCK)
+        far = [
+            jnp.dot(place[r, span], rcv[r].reshape(rows, wide), preferred_element_type=F32)
+            for r in range(ROUNDS)
+        ]
         query = qs[span].astype(F32)
         top = mloc[span]
         edges = []
         for r in range(ROUNDS):
-            score = jnp.sum(query * far[r, span], axis=1, keepdims=True)
+            score = jnp.sum(query * far[r], axis=1, keepdims=True)
             edges.append(jnp.broadcast_to(score, (BLOCK, wide)) + bias_v[r : r + 1])
         new_top = functools.reduce(jnp.maximum, edges, top)
         keep = jnp.exp(top - new_top)
@@ -499,36 +532,26 @@
         for r in range(ROUNDS):
             weight = jnp.exp(edges[r] - new_top)
             total += weight
-            blended += weight.astype(BF16).astype(F32) * far[r, span]
-        att[span] = blended / total
-
-    left = iota((half, wide), 1) < HEAD
-
-    def packed(at):
-        block = att[pl.ds(pl.multiple_of(at * own, own), own)]
-        return jnp.where(left, pltpu.roll(block[:half], HEAD, 1), block[half:]).astype(BF16)
-
-    def a_copy(source, to_at, slot_at, send):
-        return remote(
-            source, attr.at[slot_at], a_send.at[send], a_recv.at[slot_at], device(part, to_at)
-        )
-
-    order = [(k, s) for k in (4, 3, -3, 2, -2, 1, -1, 0) for s in (1, 0)]
-    owners = [2 * mate(k) + ((xh + s) % 2) for k, s in order]
-    for i, at in enumerate(owners):
-        if i < len(owners) - 1:
-            atts[i] = packed(at)
-            a_copy(atts.at[i], at, head, i).start()
-        else:
-            atts[i] = packed(at)
-
-            @pl.when(home)
-            def _():
-                attr[head] = atts[i]
-
-            @pl.when(jnp.logical_not(home))
-            def _():
-                a_copy(atts.at[i], at, head, i).start()
+            blended += weight.astype(BF16).astype(F32) * far[r]
+        attended = blended / total
+        for s in range(share):
+            i, at = len(owners), share * b + s
+            owners.append(at)
+            upper = attended[s * own : s * own + half]
+            lower = attended[s * own + half : (s + 1) * own]
+            atts[i] = jnp.where(left, pltpu.roll(upper, HEAD, 1), lower).astype(BF16)
+            if turned:
+                a_copy(i, at).start()
+            else:
+                here = jnp.logical_and(home, at == t)
+
+                @pl.when(here)
+                def _():
+                    attr[head] = atts[i]
+
+                @pl.when(jnp.logical_not(here))
+                def _():
+                    a_copy(i, at).start()
 
     for at in range(peers):
 
@@ -542,7 +565,7 @@
 
         @pl.when(jnp.logical_or(at != head, jnp.logical_not(home)))
         def _():
-            a_copy(atts.at[0], t, at, 0).wait_recv()
+            a_wait(at)
 
     tops, bottoms = [], []
     for pair in range(peers // 2):
@@ -559,18 +582,24 @@
     @pl.when(jnp.logical_not(home))
     def _():
         for c in range(CHUNKS):
-            swap_x(c).wait_send()
+            for to in range(3):
+                swap_x(c, to).wait_send()
         cross_w.wait_send()
         cross_b.wait_send()
-        a_copy(atts.at[peers - 1], owners[-1], head, peers - 1).wait_send()
 
     @pl.when(home)
     def _():
         twin_s.wait_send()
         twin_b.wait_send()
-
-    for copy in sent + weights_sent + neighbours:
+        for c in range(CHUNKS):
+            for to in range(2):
+                lead(c, to).wait_send()
+
+    for copy in sent + weights_sent:
         copy.wait_send()
+    for pair in range(ring):
+        for which in range(2):
+            n_copy(pair, which).wait_send()
 
     @pl.loop(0, parts)
     def _(i):
@@ -581,8 +610,12 @@
 
     for k in range(ring):
         hand(2 * k + core).wait_send()
-    for i in range(peers - 1):
-        a_copy(atts.at[i], owners[i], head, i).wait_send()
+    for i, at in enumerate(owners):
+
+        @pl.when(jnp.logical_or(at != t, jnp.logical_not(home)))
+        def _():
+            a_copy(i, at).wait_send()
+
     for at in range(peers):
 
         @pl.when(at != t)
@@ -612,14 +645,14 @@
     return pl.pallas_call(
         functools.partial(kernel, parts, peers),
         out_shape=jax.ShapeDtypeStruct((own, D), BF16),
-        in_specs=[pl.BlockSpec(memory_space=pl.ANY)] * 7,
+        in_specs=[pl.BlockSpec(memory_space=pltpu.HBM)] * 7,
         out_specs=pl.BlockSpec(memory_space=pltpu.VMEM),
         scratch_shapes=[
             vmem((own, D), BF16),
             vmem((1, D), F32),
             vmem((3 * HEAD, D), BF16),
             vmem((D, 3 * HEAD), BF16),
-            vmem((ROUNDS, 1), F32),
+            vmem((1, ROUNDS), F32),
             vmem((8, 128), F32),
             vmem((8, 128), F32),
             vmem((blocks_here, NEIGH), I32),
@@ -633,11 +666,9 @@
             vmem((parts, 1, ROUNDS * per), F32),
             vmem((parts, 1, ROUNDS * per), F32),
             vmem((ROUNDS * chunks, 1, 128), F32),
-            vmem((ROUNDS * chunks, 128, rows), BF16),
+            vmem((ROUNDS, rows, rows), BF16),
             vmem((parts, ROUNDS, per, wide), BF16),
             vmem((ROUNDS, parts, per, wide), BF16),
-            vmem((ROUNDS, rows, wide), F32),
-            vmem((rows, wide), F32),
             vmem((rows, wide), F32),
             vmem((rows, wide), F32),
             vmem((rows, wide), F32),
@@ -645,7 +676,7 @@
             vmem((peers, own // 2, wide), BF16),
             vmem((peers, own, D), BF16),
             dma((5,)),
-            dma((CHUNKS + 2,)),
+            dma((3 * CHUNKS + 2,)),
             dma((4,)),
             dma((8 * CHUNKS,)),
             dma((peers, CHUNKS)),
@@ -659,13 +690,13 @@
             dma((parts,)),
             dma((parts,)),
             dma((parts,)),
-            dma((2,)),
-            dma((2,)),
+            dma((2, peers // 2)),
+            dma((2, peers // 2)),
             dma((peers,)),
             dma((peers,)),
         ],
         compiler_params=pltpu.CompilerParams(
-            collective_id=0, has_side_effects=True, vmem_limit_bytes=40 * 1024 * 1024
+            collective_id=0, has_side_effects=True, vmem_limit_bytes=58 * 1024 * 1024
         ),
         cost_estimate=pl.CostEstimate(
             flops=2 * rows * D * 8 * HEAD, bytes_accessed=4 * own * D * 8, transcendentals=rows * rows
@@ -675,7 +706,7 @@
         norm_gain.reshape(1, D),
         input_weight,
         output_weight,
-        expander_bias,
+        jnp.transpose(expander_bias),
         local_blocks,
         expander_source,
     )

time: 113 us -> 78.6 us (0.70)
  the two profiles are of different devices: /device:TPU:4 before, /device:TPU:1 now
where the time goes in v3:
time: 78.6 us; the launch traced here: 78.5 us
  Pallas kernels  76.9 us (98%)
  local copies, waits for them, and re-layouts  1.57 us (2%)
    pallas_call x1, Pallas kernels, per_device(): pl.pallas_call(functools.partial(kernel, parts, peers), out_shape=jax.Sha...  76.9 us

profile of v3, /device:TPU:1, one launch (start us, length us, event | category | flops | bytes accessed | tf_op | source)
XLA Modules:
  0.0 78.5 jit_solution(11399873215318738866)
XLA Ops:
  0.0 76.9 %shard_map.73 = bf16[64,1024]{1,0:T(8,128)(2,1)} custom-call(bf16[64,1024]{1,0:T(8,128)(2,1)} %x_ref.1, f32[1,1024]{1,0:T(1,128)} %bitcast.2, bf16[192,1024]{1,0:T(8,128)(2,1)} %win_ref.1, bf16[64,1024]{1,0:T(8,128)(2,1)} %wout_ref.1, f32[1,4]{1,0:T(1,128)} %bitcast.3, s32[4,4]{1,0:T(4,128)} %blocks_ref.1, s32[4,1024]{1,0:T(4,128)} %src_ref.1), custom_call_target="tpu_custom_call" | custom-call | flops 1073741824 | bytes 2097152 | tf_op jit(solution)/shard_map/pallas_call | solution.py:645
  76.9 1.6 %copy.9 = bf16[64,1024]{1,0:T(8,128)(2,1)} copy(bf16[64,1024]{1,0:T(8,128)(2,1)} %shard_map.73) | data formatting | bytes 262144

commit v4 on v3

--- a/solution.py
+++ b/solution.py
@@ -84,6 +84,8 @@
     n_recv,
     a_send,
     a_recv,
+    token,
+    ready,
 ):
     own = x_ref.shape[0]
     rows = own * peers
@@ -107,17 +109,20 @@
     def worker(partition):
         return device(partition - partition % 2 + core, y * 2 + partition % 2)
 
-    def distance(i):
-        q, a = i // 2, i % 2
-        return 8 + 16 * a + (q // 2) * (1 - q % 2) - ((q + 1) // 2) * (q % 2)
+    planes = parts // 4
+    xl, z = p // (parts // 2), p // 2 % planes
+
+    def shifted(i, plane):
+        lo, hi = i % 4 // 2, i % 2
+        return worker((xl + lo) % 2 * (parts // 2) + plane % planes * 2 + (xh + hi) % 2)
 
     def ahead(i):
-        return worker((part + distance(i)) % parts)
+        return shifted(i, z + i // 4)
 
     def behind(i):
-        return worker((part + parts - distance(i)) % parts)
-
-    self_slot = parts - 2
+        return shifted(i, z + planes - i // 4)
+
+    self_slot = 0
     up = device(p, ((y + 1) % ring) * 2 + xh)
     down = device(p, ((y + ring - 1) % ring) * 2 + xh)
     twin = device(base + 1 - core, t)
@@ -165,14 +170,18 @@
     def greet(to):
         pl.semaphore_signal(barrier, inc=1, device_id=to, device_id_type=MESH)
 
-    for to in (up, down, twin, swap, swap_up, swap_down, cross):
+    for to in (up, down, twin, swap, swap_up, swap_down, cross, ahead(1), ahead(2), ahead(3)):
         greet(to)
-
-    @pl.loop(0, parts)
-    def _(i):
-        @pl.when(i != self_slot)
-        def _():
-            greet(ahead(i))
+    higher, lower = ahead(4), behind(4)
+    has_higher, has_lower = z < planes - 1, z > 0
+
+    @pl.when(has_higher)
+    def _():
+        greet(higher)
+
+    @pl.when(has_lower)
+    def _():
+        greet(lower)
 
     bias_load.wait()
     for r in range(ROUNDS):
@@ -185,7 +194,7 @@
         bias_v[...] = bias_out[...]
         blocks_v[...] = blocks_out[...]
 
-    pl.semaphore_wait(barrier, parts + 6)
+    pl.semaphore_wait(barrier, 10 + jnp.minimum(z, 1) + jnp.minimum(planes - 1 - z, 1))
 
     def swap_x(c, to):
         return remote(
@@ -244,6 +253,20 @@
             for to in range(2):
                 lead(c, to).start()
 
+    @pl.when(has_lower)
+    def _():
+        pl.semaphore_wait(token, 1)
+
+    @pl.when(has_higher)
+    def _():
+        pl.semaphore_signal(token, inc=1, device_id=higher, device_id_type=MESH)
+
+    @pl.loop(0, parts)
+    def _(i):
+        @pl.when(jnp.logical_and(i >= 4, i // 4 <= z))
+        def _():
+            pl.semaphore_signal(ready, inc=1, device_id=behind(i), device_id_type=MESH)
+
     for c in range(CHUNKS):
         x_wait(first, c)
     hand(first).start()
@@ -252,10 +275,13 @@
     src = src_v[...]
     owner = lax.shift_right_logical(src, rows.bit_length() - 1)
     within = (src & (rows - 1)).astype(F32)
-    gap = (part + parts - owner) & (parts - 1)
-    offset = (gap & (parts // 2 - 1)) - parts // 4
-    turn = jnp.where(offset < 0, -2 * offset - 1, 2 * offset)
-    slot = 2 * turn + lax.shift_right_logical(gap, (parts // 2).bit_length() - 1)
+    owner_plane = lax.shift_right_logical(owner, 1) & (planes - 1)
+    owner_lo = lax.shift_right_logical(owner, (parts // 2).bit_length() - 1)
+    slot = (
+        ((z + planes - owner_plane) & (planes - 1)) * 4
+        + ((owner_lo + xl) & 1) * 2
+        + ((owner + xh) & 1)
+    )
     high = jnp.floor(within * (1.0 / per))
     low = within - high * per
     slot_rows = iota((parts, rows), 0)
@@ -319,6 +345,8 @@
         qs[pl.ds(start, 2 * own)] = jnp.where(wide_lane < HEAD, query, 0.0).astype(BF16)
         inside = pl.multiple_of(pair % pairs * 2 * own, 2 * own)
         kvx[blocks_here + pair // pairs, pl.ds(inside, 2 * own)] = totals[:, HEAD:].astype(BF16)
+
+    def share_keys(pair):
         for which in range(2):
             n_copy(pair, which).start()
 
@@ -334,30 +362,34 @@
                 x_forward(above, c, down)
         hand(below).start()
         hand(above).start()
-        if k == 1:
-            @pl.loop(0, parts)
-            def _(i):
-                @pl.when(i != self_slot)
-                def _():
-                    r_copy(i, behind(i)).start()
-
-            reqr[self_slot] = reqs[self_slot]
-
-        elif k == 2:
+        if k == 2:
             local(win_ref, win_v, g_sem.at[0]).wait()
             win_t[...] = jnp.transpose(win_v[...].astype(F32)).astype(BF16)
             project(y)
-        else:
-            for near in range(1, k):
-                project(mate(-near))
-                project(mate(near))
+
+    @pl.when(has_higher)
+    def _():
+        pl.semaphore_wait(ready, (planes - 1 - z) * 4)
+
+    @pl.loop(0, parts)
+    def _(i):
+        @pl.when(i != self_slot)
+        def _():
+            r_copy(i, behind(i)).start()
+
+    reqr[self_slot] = reqs[self_slot]
+    share_keys(y)
+    for near in range(1, last - 1):
+        for pair in (mate(-near), mate(near)):
+            project(pair)
+            share_keys(pair)
     opposite = 2 * mate(last) + core
     for c in range(CHUNKS):
         x_wait(opposite, c)
     hand(opposite).start()
-    project(mate(1 - last))
-    project(mate(last - 1))
-    project(mate(last))
+    for pair in (mate(1 - last), mate(last - 1), mate(last)):
+        project(pair)
+        share_keys(pair)
 
     half = own // 2
     own_half = pl.ds(pl.multiple_of(core * half, half), half)
@@ -424,7 +456,9 @@
         got = jnp.dot(jnp.concatenate(chosen, axis=0), table, preferred_element_type=F32)
         snd[pl.ds(step * batch, batch)] = got.astype(BF16).reshape(batch, ROUNDS, per, wide)
 
-    def serve(step):
+    def serve(turn):
+        farthest = planes // 2 + (turn + 1) // 2 * (1 - turn % 2 * 2)
+        step = jnp.where(z < planes // 2, turn + planes - z, farthest + planes) % planes
         for j in range(batch):
             i = step * batch + j
 
@@ -441,12 +475,12 @@
                 e_copy(i, ahead(i)).start()
 
     quarters = 4
-    each = parts // batch // quarters
+    each = planes // quarters
     for quarter in range(quarters):
 
         @pl.loop(quarter * each, (quarter + 1) * each)
-        def _(step):
-            serve(step)
+        def _(turn):
+            serve(turn)
 
         next(weight_steps)
 
@@ -694,6 +728,8 @@
             dma((2, peers // 2)),
             dma((peers,)),
             dma((peers,)),
+            pltpu.SemaphoreType.REGULAR,
+            pltpu.SemaphoreType.REGULAR,
         ],
         compiler_params=pltpu.CompilerParams(
             collective_id=0, has_side_effects=True, vmem_limit_bytes=58 * 1024 * 1024

time: 78.6 us -> 78.8 us (level); the launches traced: 78.5 us -> 77.9 us
  no operation moved by 1% of the time
where the time goes in v4:
time: 78.8 us; the launch traced here: 77.9 us
  Pallas kernels  76.3 us (97%)
  local copies, waits for them, and re-layouts  1.57 us (2%)
    pallas_call x1, Pallas kernels, per_device(): pl.pallas_call(functools.partial(kernel, parts, peers), out_shape=jax.Sha...  76.3 us

profile of v4, /device:TPU:1, one launch (start us, length us, event | category | flops | bytes accessed | tf_op | source)
XLA Modules:
  0.0 77.9 jit_solution(16615255088249217529)
XLA Ops:
  0.0 76.3 %shard_map.73 = bf16[64,1024]{1,0:T(8,128)(2,1)} custom-call(bf16[64,1024]{1,0:T(8,128)(2,1)} %x_ref.1, f32[1,1024]{1,0:T(1,128)} %bitcast.2, bf16[192,1024]{1,0:T(8,128)(2,1)} %win_ref.1, bf16[64,1024]{1,0:T(8,128)(2,1)} %wout_ref.1, f32[1,4]{1,0:T(1,128)} %bitcast.3, s32[4,4]{1,0:T(4,128)} %blocks_ref.1, s32[4,1024]{1,0:T(4,128)} %src_ref.1), custom_call_target="tpu_custom_call" | custom-call | flops 1073741824 | bytes 2097152 | tf_op jit(solution)/shard_map/pallas_call | solution.py:679
  76.3 1.6 %copy.9 = bf16[64,1024]{1,0:T(8,128)(2,1)} copy(bf16[64,1024]{1,0:T(8,128)(2,1)} %shard_map.73) | data formatting | bytes 262144

commit v5 on v4

--- a/solution.py
+++ b/solution.py
@@ -351,46 +351,6 @@
             n_copy(pair, which).start()
 
     last = ring // 2
-    for k in range(1, last):
-        below, above = 2 * mate(-k) + core, 2 * mate(k) + core
-        for c in range(CHUNKS):
-            x_wait(below, c)
-            if k < last - 1 or c < CHUNKS // 2:
-                x_forward(below, c, up)
-            x_wait(above, c)
-            if k < last - 1 or c >= CHUNKS // 2:
-                x_forward(above, c, down)
-        hand(below).start()
-        hand(above).start()
-        if k == 2:
-            local(win_ref, win_v, g_sem.at[0]).wait()
-            win_t[...] = jnp.transpose(win_v[...].astype(F32)).astype(BF16)
-            project(y)
-
-    @pl.when(has_higher)
-    def _():
-        pl.semaphore_wait(ready, (planes - 1 - z) * 4)
-
-    @pl.loop(0, parts)
-    def _(i):
-        @pl.when(i != self_slot)
-        def _():
-            r_copy(i, behind(i)).start()
-
-    reqr[self_slot] = reqs[self_slot]
-    share_keys(y)
-    for near in range(1, last - 1):
-        for pair in (mate(-near), mate(near)):
-            project(pair)
-            share_keys(pair)
-    opposite = 2 * mate(last) + core
-    for c in range(CHUNKS):
-        x_wait(opposite, c)
-    hand(opposite).start()
-    for pair in (mate(1 - last), mate(last - 1), mate(last)):
-        project(pair)
-        share_keys(pair)
-
     half = own // 2
     own_half = pl.ds(pl.multiple_of(core * half, half), half)
     other_half = pl.ds(pl.multiple_of((1 - core) * half, half), half)
@@ -438,6 +398,49 @@
 
     weight_steps = weight_ring()
 
+    for k in range(1, last):
+        below, above = 2 * mate(-k) + core, 2 * mate(k) + core
+        for c in range(CHUNKS):
+            x_wait(below, c)
+            if k < last - 1 or c < CHUNKS // 2:
+                x_forward(below, c, up)
+            x_wait(above, c)
+            if k < last - 1 or c >= CHUNKS // 2:
+                x_forward(above, c, down)
+        hand(below).start()
+        hand(above).start()
+        if k == 2:
+            local(win_ref, win_v, g_sem.at[0]).wait()
+            win_t[...] = jnp.transpose(win_v[...].astype(F32)).astype(BF16)
+            project(y)
+
+    next(weight_steps)
+
+    @pl.when(has_higher)
+    def _():
+        pl.semaphore_wait(ready, (planes - 1 - z) * 4)
+
+    @pl.loop(0, parts)
+    def _(i):
+        @pl.when(i != self_slot)
+        def _():
+            r_copy(i, behind(i)).start()
+
+    reqr[self_slot] = reqs[self_slot]
+    share_keys(y)
+    for near in range(1, last - 1):
+        for pair in (mate(-near), mate(near)):
+            project(pair)
+            share_keys(pair)
+    opposite = 2 * mate(last) + core
+    for c in range(CHUNKS):
+        x_wait(opposite, c)
+    hand(opposite).start()
+    for pair in (mate(1 - last), mate(last - 1), mate(last)):
+        project(pair)
+        share_keys(pair)
+
+
     diagonal = iota((128, 128), 0) == iota((128, 128), 1)
     lane_index = iota((128, rows), 1).astype(F32)
 
@@ -457,8 +460,8 @@
         snd[pl.ds(step * batch, batch)] = got.astype(BF16).reshape(batch, ROUNDS, per, wide)
 
     def serve(turn):
-        farthest = planes // 2 + (turn + 1) // 2 * (1 - turn % 2 * 2)
-        step = jnp.where(z < planes // 2, turn + planes - z, farthest + planes) % planes
+        swing = (turn + 1) // 2 * (1 - turn % 2 * 2) * (1 - 2 * core)
+        step = (planes // 2 + swing + planes) % planes
         for j in range(batch):
             i = step * batch + j
 
@@ -474,25 +477,27 @@
             def _():
                 e_copy(i, ahead(i)).start()
 
-    quarters = 4
-    each = planes // quarters
-    for quarter in range(quarters):
-
-        @pl.loop(quarter * each, (quarter + 1) * each)
-        def _(turn):
-            serve(turn)
+    @pl.loop(0, 5)
+    def _(turn):
+        serve(turn)
+
+    next(weight_steps)
+
+    @pl.loop(5, planes)
+    def _(turn):
+        serve(turn)
+
+    rcv[:, self_slot] = snd[self_slot]
+
+    next(weight_steps)
+    for part_of in range(2):
+
+        @pl.loop(part_of * ROUNDS * row_chunks // 2, (part_of + 1) * ROUNDS * row_chunks // 2)
+        def _(i):
+            span = pl.ds(pl.multiple_of(i % row_chunks * 128, 128), 128)
+            place[i // row_chunks, span] = one_hot(posr[i])
 
         next(weight_steps)
-
-    rcv[:, self_slot] = snd[self_slot]
-
-    @pl.loop(0, ROUNDS * row_chunks)
-    def _(i):
-        span = pl.ds(pl.multiple_of(i % row_chunks * 128, 128), 128)
-        place[i // row_chunks, span] = one_hot(posr[i])
-
-    for _ in weight_steps:
-        pass
 
     @pl.when(jnp.logical_not(home))
     def _():
@@ -527,6 +532,8 @@
         oloc[span] = blended
         mloc[span] = jnp.broadcast_to(top, (BLOCK, wide))
         lloc[span] = jnp.broadcast_to(total, (BLOCK, wide))
+        next(weight_steps, None)
+
 
     @pl.loop(0, parts)
     def _(i):

time: 78.8 us -> 77.4 us (0.982); the launches traced: 77.9 us -> 77.3 us
  no operation moved by 1% of the time
where the time goes in v5:
time: 77.4 us; the launch traced here: 77.3 us
  Pallas kernels  75.7 us (98%)
  local copies, waits for them, and re-layouts  1.57 us (2%)
    pallas_call x1, Pallas kernels, per_device(): pl.pallas_call(functools.partial(kernel, parts, peers), out_shape=jax.Sha...  75.7 us
    unnamed x1, local copies, waits for them, and re-layouts  1.57 us

profile of v5, /device:TPU:1, one launch (start us, length us, event | category | flops | bytes accessed | tf_op | source)
XLA Modules:
  0.0 77.3 jit_solution(3038441303449371052)
XLA Ops:
  0.0 75.7 %shard_map.73 = bf16[64,1024]{1,0:T(8,128)(2,1)} custom-call(bf16[64,1024]{1,0:T(8,128)(2,1)} %x_ref.1, f32[1,1024]{1,0:T(1,128)} %bitcast.2, bf16[192,1024]{1,0:T(8,128)(2,1)} %win_ref.1, bf16[64,1024]{1,0:T(8,128)(2,1)} %wout_ref.1, f32[1,4]{1,0:T(1,128)} %bitcast.3, s32[4,4]{1,0:T(4,128)} %blocks_ref.1, s32[4,1024]{1,0:T(4,128)} %src_ref.1), custom_call_target="tpu_custom_call" | custom-call | flops 1073741824 | bytes 2097152 | tf_op jit(solution)/shard_map/pallas_call | solution.py:686
  75.7 1.6 %copy.9 = bf16[64,1024]{1,0:T(8,128)(2,1)} copy(bf16[64,1024]{1,0:T(8,128)(2,1)} %shard_map.73) | data formatting | bytes 262144

commit v6 on v5

--- a/solution.py
+++ b/solution.py
@@ -410,23 +410,25 @@
         hand(below).start()
         hand(above).start()
         if k == 2:
+
+            @pl.when(has_higher)
+            def _():
+                pl.semaphore_wait(ready, (planes - 1 - z) * 4)
+
+            @pl.loop(0, parts)
+            def _(i):
+                @pl.when(i != self_slot)
+                def _():
+                    r_copy(i, behind(i)).start()
+
+            reqr[self_slot] = reqs[self_slot]
+
             local(win_ref, win_v, g_sem.at[0]).wait()
             win_t[...] = jnp.transpose(win_v[...].astype(F32)).astype(BF16)
             project(y)
 
     next(weight_steps)
 
-    @pl.when(has_higher)
-    def _():
-        pl.semaphore_wait(ready, (planes - 1 - z) * 4)
-
-    @pl.loop(0, parts)
-    def _(i):
-        @pl.when(i != self_slot)
-        def _():
-            r_copy(i, behind(i)).start()
-
-    reqr[self_slot] = reqs[self_slot]
     share_keys(y)
     for near in range(1, last - 1):
         for pair in (mate(-near), mate(near)):

time: 77.4 us -> 77 us (level)
  no operation moved by 1% of the time
where the time goes in v6:
time: 77 us; the launch traced here: 76.8 us
  Pallas kernels  75.2 us (98%)
  local copies, waits for them, and re-layouts  1.57 us (2%)
    pallas_call x1, Pallas kernels, per_device(): pl.pallas_call(functools.partial(kernel, parts, peers), out_shape=jax.Sha...  75.2 us
    unnamed x1, local copies, waits for them, and re-layouts  1.57 us

profile of v6, /device:TPU:1, one launch (start us, length us, event | category | flops | bytes accessed | tf_op | source)
XLA Modules:
  0.0 76.8 jit_solution(13636625744493687616)
XLA Ops:
  0.0 75.2 %shard_map.73 = bf16[64,1024]{1,0:T(8,128)(2,1)} custom-call(bf16[64,1024]{1,0:T(8,128)(2,1)} %x_ref.1, f32[1,1024]{1,0:T(1,128)} %bitcast.2, bf16[192,1024]{1,0:T(8,128)(2,1)} %win_ref.1, bf16[64,1024]{1,0:T(8,128)(2,1)} %wout_ref.1, f32[1,4]{1,0:T(1,128)} %bitcast.3, s32[4,4]{1,0:T(4,128)} %blocks_ref.1, s32[4,1024]{1,0:T(4,128)} %src_ref.1), custom_call_target="tpu_custom_call" | custom-call | flops 1073741824 | bytes 2097152 | tf_op jit(solution)/shard_map/pallas_call | solution.py:688
  75.2 1.6 %copy.9 = bf16[64,1024]{1,0:T(8,128)(2,1)} copy(bf16[64,1024]{1,0:T(8,128)(2,1)} %shard_map.73) | data formatting | bytes 262144
